TPU v7x, 512 devices: a whole 4x8x8 slice. The times are simulated.
512 devices in a mesh: blk: 64 (over z_lo, y, core), uly: 8 (over x, z_hi).
Axes of the slice: x: 4, y: 8, z: 8 (z_hi: 2, z_lo: 4; z = z_hi * 4 + z_lo), core: 2. Of those that a mesh axis runs over, the one named last changes fastest.
Arguments:
- query: bfloat16 [8192, 3072], P(('blk', 'uly')), may hold values from -64 to 64
- key: bfloat16 [8192, 3072], P(('blk', 'uly')), may hold values from -64 to 64
- value: bfloat16 [8192, 3072], P(('blk', 'uly')), may hold values from -6 to 6
- tile_list: int32 [64, 32], P('blk'), may hold values from -1 to 63, as said below
Outputs:
- attended: bfloat16 [8192, 3072], P(('blk', 'uly'))
Inputs may be any that keep to these rules, and one draw needn't show every extreme that they name: `tile_list`: each row lists distinct key tiles, its own tile among them, followed by -1 in unused slots; at least 2 slots are used and some row uses all 32.
All inputs are finite; a program needn't handle non-finite values.
Results may differ from a plain program's by a relative error of at most 0.0085.
Values may be sent and summed in bfloat16 or wider, within the bound.
A program may use at most 64 MiB of HBM per device.

v0:
```python
import jax
import jax.numpy as jnp
from jax import lax
from jax.sharding import PartitionSpec as P

HEAD_DIM = 128
TILE = 128


def shifted(x, axis, by):
    length = lax.axis_size(axis)
    return lax.ppermute(x, axis, [(i, (i + by) % length) for i in range(length)])


def tile_table(tile_list, ktiles):
    tile_ids = jnp.arange(ktiles, dtype=jnp.int32)
    return jnp.any(tile_list[:, :, None] == tile_ids[None, None, :], axis=1).astype(jnp.float32)


def attend(carry, query_heads, keys, values, start, table):
    key_rows = keys.shape[0]
    query_rows = query_heads.shape[0]
    heads_loc = query_heads.shape[1] // HEAD_DIM
    column_tiles = (start + jnp.arange(key_rows, dtype=jnp.int32)) // TILE
    onehot = (column_tiles[:, None] == jnp.arange(table.shape[1], dtype=jnp.int32)[None, :]).astype(
        jnp.float32
    )
    block_allowed = jnp.dot(table, jnp.transpose(onehot))
    allowed = jnp.repeat(block_allowed, TILE, axis=0) > 0.5
    highest, denominator, numerator = carry
    query_3d = query_heads.reshape(query_rows, heads_loc, HEAD_DIM)
    keys_3d = keys.reshape(key_rows, heads_loc, HEAD_DIM)
    values_3d = values.reshape(key_rows, heads_loc, HEAD_DIM)
    scores = jnp.einsum(
        "qhd,khd->hqk", query_3d, keys_3d, preferred_element_type=jnp.float32
    ) * HEAD_DIM ** (-0.5)
    scores = jnp.where(allowed[None, :, :], scores, -jnp.inf)
    new_highest = jnp.maximum(highest, jnp.max(scores, axis=-1))
    expo = jnp.exp(scores - new_highest[:, :, None])
    rescale = jnp.exp(highest - new_highest)
    new_denominator = denominator * rescale + jnp.sum(expo, axis=-1)
    weights = expo.astype(jnp.bfloat16)
    product = jnp.einsum("hqk,khd->qhd", weights, values_3d, preferred_element_type=jnp.float32)
    new_numerator = numerator * jnp.transpose(rescale)[:, :, None] + product
    return (new_highest, new_denominator, new_numerator)


def per_device(query, key, value, tile_list):
    query_heads, key_heads, value_heads = (
        lax.all_to_all(query, "uly", split_axis=1, concat_axis=0, tiled=True),
        lax.all_to_all(key, "uly", split_axis=1, concat_axis=0, tiled=True),
        lax.all_to_all(value, "uly", split_axis=1, concat_axis=0, tiled=True),
    )
    query_rows = query_heads.shape[0]
    heads_loc = query_heads.shape[1] // HEAD_DIM
    blocks = lax.axis_size("blk")
    position = lax.axis_index("blk")
    table = tile_table(tile_list, blocks * query_rows // TILE)
    initial = (
        jnp.full((heads_loc, query_rows), -1e30, jnp.float32),
        jnp.zeros((heads_loc, query_rows), jnp.float32),
        jnp.zeros((query_rows, heads_loc, HEAD_DIM), jnp.float32),
    )
    own_state = attend(initial, query_heads, key_heads, value_heads, position * query_rows, table)

    def cycle_turn(turn_index, loop_state):
        pair, state = loop_state
        pair = shifted((pair[0], pair[1]), "blk", 1)
        source = (position - turn_index) % blocks
        state = attend(state, query_heads, pair[0], pair[1], source * query_rows, table)
        return (pair, state)

    pair, final = lax.fori_loop(1, blocks, cycle_turn, ((key_heads, value_heads), own_state))
    highest, denominator, numerator = final
    result = (numerator / jnp.transpose(denominator)[:, :, None]).astype(jnp.bfloat16)
    result = result.reshape(query_rows, heads_loc * HEAD_DIM)
    return lax.all_to_all(result, "uly", split_axis=0, concat_axis=1, tiled=True)


def solution(mesh):
    return jax.shard_map(
        per_device,
        mesh=mesh,
        in_specs=(
            P(("blk", "uly"), None),
            P(("blk", "uly"), None),
            P(("blk", "uly"), None),
            P("blk", None),
        ),
        out_specs=P(("blk", "uly"), None),
        check_vma=False,
    )
```

profile of v0, /device:TPU:1, one launch (start us, length us, event | category | flops | bytes accessed | tf_op | source)
XLA Modules:
  0.0 821.3 jit_solution(4968182883770960775)
XLA Ops:
  1.5 13.4 %all-to-all-start.2 = ((bf16[16,8,384]{2,0,1:T(8,128)(2,1)}), bf16[16,8,384]{2,0,1:T(8,128)(2,1)S(1)}, u32[]{:S(2)}, u32[]{:S(2)}) async-start(bf16[16,8,384]{2,0,1:T(8,128)(2,1)} %bitcast.58), calls=%async_computation.2 | async-start | bytes 196608 | tf_op jit(solution)/shard_map/all_to_all | solution.py:50
  17.5 6.8 all-to-all-done.2
  27.7 9.2 %all-to-all-done = bf16[16,8,384]{2,0,1:T(8,128)(2,1)S(1)} async-done(((bf16[16,8,384]{2,0,1:T(8,128)(2,1)}), bf16[16,8,384]{2,0,1:T(8,128)(2,1)S(1)}, u32[]{:S(2)}, u32[]{:S(2)}) %all-to-all-start) | async-done | bytes 98336 | tf_op jit(solution)/shard_map/all_to_all | solution.py:51
  40.6 8.9 %all-to-all-done.1 = bf16[16,8,384]{2,0,1:T(8,128)(2,1)S(1)} async-done(((bf16[16,8,384]{2,0,1:T(8,128)(2,1)}), bf16[16,8,384]{2,0,1:T(8,128)(2,1)S(1)}, u32[]{:S(2)}, u32[]{:S(2)}) %all-to-all-start.1) | async-done | bytes 98336 | tf_op jit(solution)/shard_map/all_to_all | solution.py:52
  50.2 758.5 %while.23 = (s32[]{:T(128)}, bf16[128,384]{0,1:T(8,128)(2,1)S(1)}, bf16[128,384]{0,1:T(8,128)(2,1)S(1)}, f32[3,128]{1,0:T(4,128)S(1)}, f32[3,128]{1,0:T(4,128)S(...) while((s32[]{:T(128)}, bf16[128,384]{0,1:T(8,128)(2,1)S(1)}, ...), condition=%wide.region_6.7_spmd, body=%wide.region_3.6_spmd.sunk | while | flops 25636112 | bytes 2483934 | solution.py:73
  50.2 7.5 collective-permute-start
  87.8 5.7 collective-permute-done
  99.8 5.7 collective-permute-done
  111.9 5.7 collective-permute-done
  124.0 5.7 collective-permute-done
  136.1 5.7 collective-permute-done
  148.2 5.7 collective-permute-done
  160.2 5.7 collective-permute-done
  172.3 5.7 collective-permute-done
  184.4 5.7 collective-permute-done
  196.5 5.7 collective-permute-done
  208.6 5.7 collective-permute-done
  220.7 5.7 collective-permute-done
  232.7 5.7 collective-permute-done
  244.8 5.7 collective-permute-done
  256.9 5.7 collective-permute-done
  269.0 5.7 collective-permute-done
  281.1 5.7 collective-permute-done
  293.1 5.7 collective-permute-done
  305.2 5.7 collective-permute-done
  317.3 5.7 collective-permute-done
  329.4 5.7 collective-permute-done
  341.5 5.7 collective-permute-done
  353.5 5.7 collective-permute-done
  365.6 5.7 collective-permute-done
  377.7 5.7 collective-permute-done
  389.8 5.7 collective-permute-done
  401.9 5.7 collective-permute-done
  413.9 5.7 collective-permute-done
  426.0 5.7 collective-permute-done
  438.1 5.7 collective-permute-done
  450.2 5.7 collective-permute-done
  462.3 5.7 collective-permute-done
  474.4 5.7 collective-permute-done
  486.4 5.7 collective-permute-done
  498.5 5.7 collective-permute-done
  510.6 5.7 collective-permute-done
  522.7 5.7 collective-permute-done
  534.8 5.7 collective-permute-done
  546.8 5.7 collective-permute-done
  558.9 5.7 collective-permute-done
  571.0 5.7 collective-permute-done
  583.1 5.7 collective-permute-done
  595.2 5.7 collective-permute-done
  607.2 5.7 collective-permute-done
  619.3 5.7 collective-permute-done
  631.4 5.7 collective-permute-done
  643.5 5.7 collective-permute-done
  655.6 5.7 collective-permute-done
  667.6 5.7 collective-permute-done
  679.7 5.7 collective-permute-done
  691.8 5.7 collective-permute-done
  703.9 5.7 collective-permute-done
  728.0 5.8 collective-permute-done
  740.2 5.7 collective-permute-done
  764.4 5.7 collective-permute-done
  788.6 5.7 collective-permute-done
  800.6 5.7 collective-permute-done
  808.9 11.7 %all_to_all.76 = bf16[8,16,384]{2,1,0:T(8,128)(2,1)S(1)} all-to-all(bf16[8,16,384]{2,1,0:T(8,128)(2,1)S(1)} %all_to_all.68), channel_id=1, replica_groups=mesh['blk'=64,'uly'=8] {'uly'}, dimensions={0} | all-to-all | bytes 196608 | tf_op jit(solution)/shard_map/all_to_all | solution.py:77
  (854 shorter events, 430.4 us)
Async XLA Ops:
  1.5 22.8 %all-to-all-start.2 = ((bf16[16,8,384]{2,0,1:T(8,128)(2,1)}), bf16[16,8,384]{2,0,1:T(8,128)(2,1)S(1)}, u32[]{:S(2)}, u32[]{:S(2)}) async-start(bf16[16,8,384]{2,0,1:T(8,128)(2,1)} %bitcast.58), calls=%async_computation.2 | async-start | bytes 196608 | tf_op jit(solution)/shard_map/all_to_all | solution.py:50
  24.3 12.6 %all-to-all-start = ((bf16[16,8,384]{2,0,1:T(8,128)(2,1)}), bf16[16,8,384]{2,0,1:T(8,128)(2,1)S(1)}, u32[]{:S(2)}, u32[]{:S(2)}) async-start(bf16[16,8,384]{2,0,1:T(8,128)(2,1)} %bitcast.60), calls=%async_computation | async-start | bytes 196608 | tf_op jit(solution)/shard_map/all_to_all | solution.py:51
  36.9 12.6 %all-to-all-start.1 = ((bf16[16,8,384]{2,0,1:T(8,128)(2,1)}), bf16[16,8,384]{2,0,1:T(8,128)(2,1)S(1)}, u32[]{:S(2)}, u32[]{:S(2)}) async-start(bf16[16,8,384]{2,0,1:T(8,128)(2,1)} %bitcast.59), calls=%async_computation.1 | async-start | bytes 196608 | tf_op jit(solution)/shard_map/all_to_all | solution.py:52
  71.6 9.8 %collective-permute-start = (bf16[128,384]{0,1:T(8,128)(2,1)S(1)}, bf16[128,384]{0,1:T(8,128)(2,1)S(1)}, u32[]{:S(2)}, u32[]{:S(2)}) collective-permute-start(bf16[128,384]{0,1:T(8,128)(2,1)S(1)} %get-tuple-element.371), channel_id=1, source_target_pairs={{0,8},{8,16},{16,24},{24,32},{32,40},{40,48},{48,56},{56,64},{64,7... | collective-permute-start | bytes 294920 | tf_op jit(solution)/shard_map/while/body/eval_jaxpr/ppermute | solution.py:12
  95.7 9.8 %collective-permute-start = (bf16[128,384]{0,1:T(8,128)(2,1)S(1)}, bf16[128,384]{0,1:T(8,128)(2,1)S(1)}, u32[]{:S(2)}, u32[]{:S(2)}) collective-permute-start(bf16[128,384]{0,1:T(8,128)(2,1)S(1)} %get-tuple-element.371), channel_id=1, source_target_pairs={{0,8},{8,16},{16,24},{24,32},{32,40},{40,48},{48,56},{56,64},{64,7... | collective-permute-start | bytes 294920 | tf_op jit(solution)/shard_map/while/body/eval_jaxpr/ppermute | solution.py:12
  97.7 9.8 %collective-permute-start.1 = (bf16[128,384]{0,1:T(8,128)(2,1)S(1)}, bf16[128,384]{0,1:T(8,128)(2,1)S(1)}, u32[]{:S(2)}, u32[]{:S(2)}) collective-permute-start(bf16[128,384]{0,1:T(8,128)(2,1)S(1)} %get-tuple-element.372), channel_id=1, source_target_pairs={{0,8},{8,16},{16,24},{24,32},{32,40},{40,48},{48,56},{56,64},{64,7... | collective-permute-start | bytes 294920 | tf_op jit(solution)/shard_map/while/body/eval_jaxpr/ppermute | solution.py:12
  119.9 9.8 %collective-permute-start = (bf16[128,384]{0,1:T(8,128)(2,1)S(1)}, bf16[128,384]{0,1:T(8,128)(2,1)S(1)}, u32[]{:S(2)}, u32[]{:S(2)}) collective-permute-start(bf16[128,384]{0,1:T(8,128)(2,1)S(1)} %get-tuple-element.371), channel_id=1, source_target_pairs={{0,8},{8,16},{16,24},{24,32},{32,40},{40,48},{48,56},{56,64},{64,7... | collective-permute-start | bytes 294920 | tf_op jit(solution)/shard_map/while/body/eval_jaxpr/ppermute | solution.py:12
  121.8 9.8 %collective-permute-start.1 = (bf16[128,384]{0,1:T(8,128)(2,1)S(1)}, bf16[128,384]{0,1:T(8,128)(2,1)S(1)}, u32[]{:S(2)}, u32[]{:S(2)}) collective-permute-start(bf16[128,384]{0,1:T(8,128)(2,1)S(1)} %get-tuple-element.372), channel_id=1, source_target_pairs={{0,8},{8,16},{16,24},{24,32},{32,40},{40,48},{48,56},{56,64},{64,7... | collective-permute-start | bytes 294920 | tf_op jit(solution)/shard_map/while/body/eval_jaxpr/ppermute | solution.py:12
  132.0 9.8 %collective-permute-start = (bf16[128,384]{0,1:T(8,128)(2,1)S(1)}, bf16[128,384]{0,1:T(8,128)(2,1)S(1)}, u32[]{:S(2)}, u32[]{:S(2)}) collective-permute-start(bf16[128,384]{0,1:T(8,128)(2,1)S(1)} %get-tuple-element.371), channel_id=1, source_target_pairs={{0,8},{8,16},{16,24},{24,32},{32,40},{40,48},{48,56},{56,64},{64,7... | collective-permute-start | bytes 294920 | tf_op jit(solution)/shard_map/while/body/eval_jaxpr/ppermute | solution.py:12
  133.9 9.8 %collective-permute-start.1 = (bf16[128,384]{0,1:T(8,128)(2,1)S(1)}, bf16[128,384]{0,1:T(8,128)(2,1)S(1)}, u32[]{:S(2)}, u32[]{:S(2)}) collective-permute-start(bf16[128,384]{0,1:T(8,128)(2,1)S(1)} %get-tuple-element.372), channel_id=1, source_target_pairs={{0,8},{8,16},{16,24},{24,32},{32,40},{40,48},{48,56},{56,64},{64,7... | collective-permute-start | bytes 294920 | tf_op jit(solution)/shard_map/while/body/eval_jaxpr/ppermute | solution.py:12
  156.2 9.8 %collective-permute-start = (bf16[128,384]{0,1:T(8,128)(2,1)S(1)}, bf16[128,384]{0,1:T(8,128)(2,1)S(1)}, u32[]{:S(2)}, u32[]{:S(2)}) collective-permute-start(bf16[128,384]{0,1:T(8,128)(2,1)S(1)} %get-tuple-element.371), channel_id=1, source_target_pairs={{0,8},{8,16},{16,24},{24,32},{32,40},{40,48},{48,56},{56,64},{64,7... | collective-permute-start | bytes 294920 | tf_op jit(solution)/shard_map/while/body/eval_jaxpr/ppermute | solution.py:12
  158.1 9.8 %collective-permute-start.1 = (bf16[128,384]{0,1:T(8,128)(2,1)S(1)}, bf16[128,384]{0,1:T(8,128)(2,1)S(1)}, u32[]{:S(2)}, u32[]{:S(2)}) collective-permute-start(bf16[128,384]{0,1:T(8,128)(2,1)S(1)} %get-tuple-element.372), channel_id=1, source_target_pairs={{0,8},{8,16},{16,24},{24,32},{32,40},{40,48},{48,56},{56,64},{64,7... | collective-permute-start | bytes 294920 | tf_op jit(solution)/shard_map/while/body/eval_jaxpr/ppermute | solution.py:12
  180.3 9.8 %collective-permute-start = (bf16[128,384]{0,1:T(8,128)(2,1)S(1)}, bf16[128,384]{0,1:T(8,128)(2,1)S(1)}, u32[]{:S(2)}, u32[]{:S(2)}) collective-permute-start(bf16[128,384]{0,1:T(8,128)(2,1)S(1)} %get-tuple-element.371), channel_id=1, source_target_pairs={{0,8},{8,16},{16,24},{24,32},{32,40},{40,48},{48,56},{56,64},{64,7... | collective-permute-start | bytes 294920 | tf_op jit(solution)/shard_map/while/body/eval_jaxpr/ppermute | solution.py:12
  182.2 9.8 %collective-permute-start.1 = (bf16[128,384]{0,1:T(8,128)(2,1)S(1)}, bf16[128,384]{0,1:T(8,128)(2,1)S(1)}, u32[]{:S(2)}, u32[]{:S(2)}) collective-permute-start(bf16[128,384]{0,1:T(8,128)(2,1)S(1)} %get-tuple-element.372), channel_id=1, source_target_pairs={{0,8},{8,16},{16,24},{24,32},{32,40},{40,48},{48,56},{56,64},{64,7... | collective-permute-start | bytes 294920 | tf_op jit(solution)/shard_map/while/body/eval_jaxpr/ppermute | solution.py:12
  192.4 9.8 %collective-permute-start = (bf16[128,384]{0,1:T(8,128)(2,1)S(1)}, bf16[128,384]{0,1:T(8,128)(2,1)S(1)}, u32[]{:S(2)}, u32[]{:S(2)}) collective-permute-start(bf16[128,384]{0,1:T(8,128)(2,1)S(1)} %get-tuple-element.371), channel_id=1, source_target_pairs={{0,8},{8,16},{16,24},{24,32},{32,40},{40,48},{48,56},{56,64},{64,7... | collective-permute-start | bytes 294920 | tf_op jit(solution)/shard_map/while/body/eval_jaxpr/ppermute | solution.py:12
  194.3 9.8 %collective-permute-start.1 = (bf16[128,384]{0,1:T(8,128)(2,1)S(1)}, bf16[128,384]{0,1:T(8,128)(2,1)S(1)}, u32[]{:S(2)}, u32[]{:S(2)}) collective-permute-start(bf16[128,384]{0,1:T(8,128)(2,1)S(1)} %get-tuple-element.372), channel_id=1, source_target_pairs={{0,8},{8,16},{16,24},{24,32},{32,40},{40,48},{48,56},{56,64},{64,7... | collective-permute-start | bytes 294920 | tf_op jit(solution)/shard_map/while/body/eval_jaxpr/ppermute | solution.py:12
  216.6 9.8 %collective-permute-start = (bf16[128,384]{0,1:T(8,128)(2,1)S(1)}, bf16[128,384]{0,1:T(8,128)(2,1)S(1)}, u32[]{:S(2)}, u32[]{:S(2)}) collective-permute-start(bf16[128,384]{0,1:T(8,128)(2,1)S(1)} %get-tuple-element.371), channel_id=1, source_target_pairs={{0,8},{8,16},{16,24},{24,32},{32,40},{40,48},{48,56},{56,64},{64,7... | collective-permute-start | bytes 294920 | tf_op jit(solution)/shard_map/while/body/eval_jaxpr/ppermute | solution.py:12
  218.5 9.8 %collective-permute-start.1 = (bf16[128,384]{0,1:T(8,128)(2,1)S(1)}, bf16[128,384]{0,1:T(8,128)(2,1)S(1)}, u32[]{:S(2)}, u32[]{:S(2)}) collective-permute-start(bf16[128,384]{0,1:T(8,128)(2,1)S(1)} %get-tuple-element.372), channel_id=1, source_target_pairs={{0,8},{8,16},{16,24},{24,32},{32,40},{40,48},{48,56},{56,64},{64,7... | collective-permute-start | bytes 294920 | tf_op jit(solution)/shard_map/while/body/eval_jaxpr/ppermute | solution.py:12
  240.7 9.8 %collective-permute-start = (bf16[128,384]{0,1:T(8,128)(2,1)S(1)}, bf16[128,384]{0,1:T(8,128)(2,1)S(1)}, u32[]{:S(2)}, u32[]{:S(2)}) collective-permute-start(bf16[128,384]{0,1:T(8,128)(2,1)S(1)} %get-tuple-element.371), channel_id=1, source_target_pairs={{0,8},{8,16},{16,24},{24,32},{32,40},{40,48},{48,56},{56,64},{64,7... | collective-permute-start | bytes 294920 | tf_op jit(solution)/shard_map/while/body/eval_jaxpr/ppermute | solution.py:12
  242.6 9.8 %collective-permute-start.1 = (bf16[128,384]{0,1:T(8,128)(2,1)S(1)}, bf16[128,384]{0,1:T(8,128)(2,1)S(1)}, u32[]{:S(2)}, u32[]{:S(2)}) collective-permute-start(bf16[128,384]{0,1:T(8,128)(2,1)S(1)} %get-tuple-element.372), channel_id=1, source_target_pairs={{0,8},{8,16},{16,24},{24,32},{32,40},{40,48},{48,56},{56,64},{64,7... | collective-permute-start | bytes 294920 | tf_op jit(solution)/shard_map/while/body/eval_jaxpr/ppermute | solution.py:12
  252.8 9.8 %collective-permute-start = (bf16[128,384]{0,1:T(8,128)(2,1)S(1)}, bf16[128,384]{0,1:T(8,128)(2,1)S(1)}, u32[]{:S(2)}, u32[]{:S(2)}) collective-permute-start(bf16[128,384]{0,1:T(8,128)(2,1)S(1)} %get-tuple-element.371), channel_id=1, source_target_pairs={{0,8},{8,16},{16,24},{24,32},{32,40},{40,48},{48,56},{56,64},{64,7... | collective-permute-start | bytes 294920 | tf_op jit(solution)/shard_map/while/body/eval_jaxpr/ppermute | solution.py:12
  254.7 9.8 %collective-permute-start.1 = (bf16[128,384]{0,1:T(8,128)(2,1)S(1)}, bf16[128,384]{0,1:T(8,128)(2,1)S(1)}, u32[]{:S(2)}, u32[]{:S(2)}) collective-permute-start(bf16[128,384]{0,1:T(8,128)(2,1)S(1)} %get-tuple-element.372), channel_id=1, source_target_pairs={{0,8},{8,16},{16,24},{24,32},{32,40},{40,48},{48,56},{56,64},{64,7... | collective-permute-start | bytes 294920 | tf_op jit(solution)/shard_map/while/body/eval_jaxpr/ppermute | solution.py:12
  277.0 9.8 %collective-permute-start = (bf16[128,384]{0,1:T(8,128)(2,1)S(1)}, bf16[128,384]{0,1:T(8,128)(2,1)S(1)}, u32[]{:S(2)}, u32[]{:S(2)}) collective-permute-start(bf16[128,384]{0,1:T(8,128)(2,1)S(1)} %get-tuple-element.371), channel_id=1, source_target_pairs={{0,8},{8,16},{16,24},{24,32},{32,40},{40,48},{48,56},{56,64},{64,7... | collective-permute-start | bytes 294920 | tf_op jit(solution)/shard_map/while/body/eval_jaxpr/ppermute | solution.py:12
  278.9 9.8 %collective-permute-start.1 = (bf16[128,384]{0,1:T(8,128)(2,1)S(1)}, bf16[128,384]{0,1:T(8,128)(2,1)S(1)}, u32[]{:S(2)}, u32[]{:S(2)}) collective-permute-start(bf16[128,384]{0,1:T(8,128)(2,1)S(1)} %get-tuple-element.372), channel_id=1, source_target_pairs={{0,8},{8,16},{16,24},{24,32},{32,40},{40,48},{48,56},{56,64},{64,7... | collective-permute-start | bytes 294920 | tf_op jit(solution)/shard_map/while/body/eval_jaxpr/ppermute | solution.py:12
  301.1 9.8 %collective-permute-start = (bf16[128,384]{0,1:T(8,128)(2,1)S(1)}, bf16[128,384]{0,1:T(8,128)(2,1)S(1)}, u32[]{:S(2)}, u32[]{:S(2)}) collective-permute-start(bf16[128,384]{0,1:T(8,128)(2,1)S(1)} %get-tuple-element.371), channel_id=1, source_target_pairs={{0,8},{8,16},{16,24},{24,32},{32,40},{40,48},{48,56},{56,64},{64,7... | collective-permute-start | bytes 294920 | tf_op jit(solution)/shard_map/while/body/eval_jaxpr/ppermute | solution.py:12
  303.0 9.8 %collective-permute-start.1 = (bf16[128,384]{0,1:T(8,128)(2,1)S(1)}, bf16[128,384]{0,1:T(8,128)(2,1)S(1)}, u32[]{:S(2)}, u32[]{:S(2)}) collective-permute-start(bf16[128,384]{0,1:T(8,128)(2,1)S(1)} %get-tuple-element.372), channel_id=1, source_target_pairs={{0,8},{8,16},{16,24},{24,32},{32,40},{40,48},{48,56},{56,64},{64,7... | collective-permute-start | bytes 294920 | tf_op jit(solution)/shard_map/while/body/eval_jaxpr/ppermute | solution.py:12
  313.2 9.8 %collective-permute-start = (bf16[128,384]{0,1:T(8,128)(2,1)S(1)}, bf16[128,384]{0,1:T(8,128)(2,1)S(1)}, u32[]{:S(2)}, u32[]{:S(2)}) collective-permute-start(bf16[128,384]{0,1:T(8,128)(2,1)S(1)} %get-tuple-element.371), channel_id=1, source_target_pairs={{0,8},{8,16},{16,24},{24,32},{32,40},{40,48},{48,56},{56,64},{64,7... | collective-permute-start | bytes 294920 | tf_op jit(solution)/shard_map/while/body/eval_jaxpr/ppermute | solution.py:12
  315.1 9.8 %collective-permute-start.1 = (bf16[128,384]{0,1:T(8,128)(2,1)S(1)}, bf16[128,384]{0,1:T(8,128)(2,1)S(1)}, u32[]{:S(2)}, u32[]{:S(2)}) collective-permute-start(bf16[128,384]{0,1:T(8,128)(2,1)S(1)} %get-tuple-element.372), channel_id=1, source_target_pairs={{0,8},{8,16},{16,24},{24,32},{32,40},{40,48},{48,56},{56,64},{64,7... | collective-permute-start | bytes 294920 | tf_op jit(solution)/shard_map/while/body/eval_jaxpr/ppermute | solution.py:12
  337.4 9.8 %collective-permute-start = (bf16[128,384]{0,1:T(8,128)(2,1)S(1)}, bf16[128,384]{0,1:T(8,128)(2,1)S(1)}, u32[]{:S(2)}, u32[]{:S(2)}) collective-permute-start(bf16[128,384]{0,1:T(8,128)(2,1)S(1)} %get-tuple-element.371), channel_id=1, source_target_pairs={{0,8},{8,16},{16,24},{24,32},{32,40},{40,48},{48,56},{56,64},{64,7... | collective-permute-start | bytes 294920 | tf_op jit(solution)/shard_map/while/body/eval_jaxpr/ppermute | solution.py:12
  339.3 9.8 %collective-permute-start.1 = (bf16[128,384]{0,1:T(8,128)(2,1)S(1)}, bf16[128,384]{0,1:T(8,128)(2,1)S(1)}, u32[]{:S(2)}, u32[]{:S(2)}) collective-permute-start(bf16[128,384]{0,1:T(8,128)(2,1)S(1)} %get-tuple-element.372), channel_id=1, source_target_pairs={{0,8},{8,16},{16,24},{24,32},{32,40},{40,48},{48,56},{56,64},{64,7... | collective-permute-start | bytes 294920 | tf_op jit(solution)/shard_map/while/body/eval_jaxpr/ppermute | solution.py:12
  361.5 9.8 %collective-permute-start = (bf16[128,384]{0,1:T(8,128)(2,1)S(1)}, bf16[128,384]{0,1:T(8,128)(2,1)S(1)}, u32[]{:S(2)}, u32[]{:S(2)}) collective-permute-start(bf16[128,384]{0,1:T(8,128)(2,1)S(1)} %get-tuple-element.371), channel_id=1, source_target_pairs={{0,8},{8,16},{16,24},{24,32},{32,40},{40,48},{48,56},{56,64},{64,7... | collective-permute-start | bytes 294920 | tf_op jit(solution)/shard_map/while/body/eval_jaxpr/ppermute | solution.py:12
  363.5 9.8 %collective-permute-start.1 = (bf16[128,384]{0,1:T(8,128)(2,1)S(1)}, bf16[128,384]{0,1:T(8,128)(2,1)S(1)}, u32[]{:S(2)}, u32[]{:S(2)}) collective-permute-start(bf16[128,384]{0,1:T(8,128)(2,1)S(1)} %get-tuple-element.372), channel_id=1, source_target_pairs={{0,8},{8,16},{16,24},{24,32},{32,40},{40,48},{48,56},{56,64},{64,7... | collective-permute-start | bytes 294920 | tf_op jit(solution)/shard_map/while/body/eval_jaxpr/ppermute | solution.py:12
  373.6 9.8 %collective-permute-start = (bf16[128,384]{0,1:T(8,128)(2,1)S(1)}, bf16[128,384]{0,1:T(8,128)(2,1)S(1)}, u32[]{:S(2)}, u32[]{:S(2)}) collective-permute-start(bf16[128,384]{0,1:T(8,128)(2,1)S(1)} %get-tuple-element.371), channel_id=1, source_target_pairs={{0,8},{8,16},{16,24},{24,32},{32,40},{40,48},{48,56},{56,64},{64,7... | collective-permute-start | bytes 294920 | tf_op jit(solution)/shard_map/while/body/eval_jaxpr/ppermute | solution.py:12
  375.5 9.8 %collective-permute-start.1 = (bf16[128,384]{0,1:T(8,128)(2,1)S(1)}, bf16[128,384]{0,1:T(8,128)(2,1)S(1)}, u32[]{:S(2)}, u32[]{:S(2)}) collective-permute-start(bf16[128,384]{0,1:T(8,128)(2,1)S(1)} %get-tuple-element.372), channel_id=1, source_target_pairs={{0,8},{8,16},{16,24},{24,32},{32,40},{40,48},{48,56},{56,64},{64,7... | collective-permute-start | bytes 294920 | tf_op jit(solution)/shard_map/while/body/eval_jaxpr/ppermute | solution.py:12
  397.8 9.8 %collective-permute-start = (bf16[128,384]{0,1:T(8,128)(2,1)S(1)}, bf16[128,384]{0,1:T(8,128)(2,1)S(1)}, u32[]{:S(2)}, u32[]{:S(2)}) collective-permute-start(bf16[128,384]{0,1:T(8,128)(2,1)S(1)} %get-tuple-element.371), channel_id=1, source_target_pairs={{0,8},{8,16},{16,24},{24,32},{32,40},{40,48},{48,56},{56,64},{64,7... | collective-permute-start | bytes 294920 | tf_op jit(solution)/shard_map/while/body/eval_jaxpr/ppermute | solution.py:12
  399.7 9.8 %collective-permute-start.1 = (bf16[128,384]{0,1:T(8,128)(2,1)S(1)}, bf16[128,384]{0,1:T(8,128)(2,1)S(1)}, u32[]{:S(2)}, u32[]{:S(2)}) collective-permute-start(bf16[128,384]{0,1:T(8,128)(2,1)S(1)} %get-tuple-element.372), channel_id=1, source_target_pairs={{0,8},{8,16},{16,24},{24,32},{32,40},{40,48},{48,56},{56,64},{64,7... | collective-permute-start | bytes 294920 | tf_op jit(solution)/shard_map/while/body/eval_jaxpr/ppermute | solution.py:12
  421.9 9.8 %collective-permute-start = (bf16[128,384]{0,1:T(8,128)(2,1)S(1)}, bf16[128,384]{0,1:T(8,128)(2,1)S(1)}, u32[]{:S(2)}, u32[]{:S(2)}) collective-permute-start(bf16[128,384]{0,1:T(8,128)(2,1)S(1)} %get-tuple-element.371), channel_id=1, source_target_pairs={{0,8},{8,16},{16,24},{24,32},{32,40},{40,48},{48,56},{56,64},{64,7... | collective-permute-start | bytes 294920 | tf_op jit(solution)/shard_map/while/body/eval_jaxpr/ppermute | solution.py:12
  423.9 9.8 %collective-permute-start.1 = (bf16[128,384]{0,1:T(8,128)(2,1)S(1)}, bf16[128,384]{0,1:T(8,128)(2,1)S(1)}, u32[]{:S(2)}, u32[]{:S(2)}) collective-permute-start(bf16[128,384]{0,1:T(8,128)(2,1)S(1)} %get-tuple-element.372), channel_id=1, source_target_pairs={{0,8},{8,16},{16,24},{24,32},{32,40},{40,48},{48,56},{56,64},{64,7... | collective-permute-start | bytes 294920 | tf_op jit(solution)/shard_map/while/body/eval_jaxpr/ppermute | solution.py:12
  434.0 9.8 %collective-permute-start = (bf16[128,384]{0,1:T(8,128)(2,1)S(1)}, bf16[128,384]{0,1:T(8,128)(2,1)S(1)}, u32[]{:S(2)}, u32[]{:S(2)}) collective-permute-start(bf16[128,384]{0,1:T(8,128)(2,1)S(1)} %get-tuple-element.371), channel_id=1, source_target_pairs={{0,8},{8,16},{16,24},{24,32},{32,40},{40,48},{48,56},{56,64},{64,7... | collective-permute-start | bytes 294920 | tf_op jit(solution)/shard_map/while/body/eval_jaxpr/ppermute | solution.py:12
  435.9 9.8 %collective-permute-start.1 = (bf16[128,384]{0,1:T(8,128)(2,1)S(1)}, bf16[128,384]{0,1:T(8,128)(2,1)S(1)}, u32[]{:S(2)}, u32[]{:S(2)}) collective-permute-start(bf16[128,384]{0,1:T(8,128)(2,1)S(1)} %get-tuple-element.372), channel_id=1, source_target_pairs={{0,8},{8,16},{16,24},{24,32},{32,40},{40,48},{48,56},{56,64},{64,7... | collective-permute-start | bytes 294920 | tf_op jit(solution)/shard_map/while/body/eval_jaxpr/ppermute | solution.py:12
  458.2 9.8 %collective-permute-start = (bf16[128,384]{0,1:T(8,128)(2,1)S(1)}, bf16[128,384]{0,1:T(8,128)(2,1)S(1)}, u32[]{:S(2)}, u32[]{:S(2)}) collective-permute-start(bf16[128,384]{0,1:T(8,128)(2,1)S(1)} %get-tuple-element.371), channel_id=1, source_target_pairs={{0,8},{8,16},{16,24},{24,32},{32,40},{40,48},{48,56},{56,64},{64,7... | collective-permute-start | bytes 294920 | tf_op jit(solution)/shard_map/while/body/eval_jaxpr/ppermute | solution.py:12
  460.1 9.8 %collective-permute-start.1 = (bf16[128,384]{0,1:T(8,128)(2,1)S(1)}, bf16[128,384]{0,1:T(8,128)(2,1)S(1)}, u32[]{:S(2)}, u32[]{:S(2)}) collective-permute-start(bf16[128,384]{0,1:T(8,128)(2,1)S(1)} %get-tuple-element.372), channel_id=1, source_target_pairs={{0,8},{8,16},{16,24},{24,32},{32,40},{40,48},{48,56},{56,64},{64,7... | collective-permute-start | bytes 294920 | tf_op jit(solution)/shard_map/while/body/eval_jaxpr/ppermute | solution.py:12
  482.3 9.8 %collective-permute-start = (bf16[128,384]{0,1:T(8,128)(2,1)S(1)}, bf16[128,384]{0,1:T(8,128)(2,1)S(1)}, u32[]{:S(2)}, u32[]{:S(2)}) collective-permute-start(bf16[128,384]{0,1:T(8,128)(2,1)S(1)} %get-tuple-element.371), channel_id=1, source_target_pairs={{0,8},{8,16},{16,24},{24,32},{32,40},{40,48},{48,56},{56,64},{64,7... | collective-permute-start | bytes 294920 | tf_op jit(solution)/shard_map/while/body/eval_jaxpr/ppermute | solution.py:12
  484.3 9.8 %collective-permute-start.1 = (bf16[128,384]{0,1:T(8,128)(2,1)S(1)}, bf16[128,384]{0,1:T(8,128)(2,1)S(1)}, u32[]{:S(2)}, u32[]{:S(2)}) collective-permute-start(bf16[128,384]{0,1:T(8,128)(2,1)S(1)} %get-tuple-element.372), channel_id=1, source_target_pairs={{0,8},{8,16},{16,24},{24,32},{32,40},{40,48},{48,56},{56,64},{64,7... | collective-permute-start | bytes 294920 | tf_op jit(solution)/shard_map/while/body/eval_jaxpr/ppermute | solution.py:12
  494.4 9.8 %collective-permute-start = (bf16[128,384]{0,1:T(8,128)(2,1)S(1)}, bf16[128,384]{0,1:T(8,128)(2,1)S(1)}, u32[]{:S(2)}, u32[]{:S(2)}) collective-permute-start(bf16[128,384]{0,1:T(8,128)(2,1)S(1)} %get-tuple-element.371), channel_id=1, source_target_pairs={{0,8},{8,16},{16,24},{24,32},{32,40},{40,48},{48,56},{56,64},{64,7... | collective-permute-start | bytes 294920 | tf_op jit(solution)/shard_map/while/body/eval_jaxpr/ppermute | solution.py:12
  496.3 9.8 %collective-permute-start.1 = (bf16[128,384]{0,1:T(8,128)(2,1)S(1)}, bf16[128,384]{0,1:T(8,128)(2,1)S(1)}, u32[]{:S(2)}, u32[]{:S(2)}) collective-permute-start(bf16[128,384]{0,1:T(8,128)(2,1)S(1)} %get-tuple-element.372), channel_id=1, source_target_pairs={{0,8},{8,16},{16,24},{24,32},{32,40},{40,48},{48,56},{56,64},{64,7... | collective-permute-start | bytes 294920 | tf_op jit(solution)/shard_map/while/body/eval_jaxpr/ppermute | solution.py:12
  518.6 9.8 %collective-permute-start = (bf16[128,384]{0,1:T(8,128)(2,1)S(1)}, bf16[128,384]{0,1:T(8,128)(2,1)S(1)}, u32[]{:S(2)}, u32[]{:S(2)}) collective-permute-start(bf16[128,384]{0,1:T(8,128)(2,1)S(1)} %get-tuple-element.371), channel_id=1, source_target_pairs={{0,8},{8,16},{16,24},{24,32},{32,40},{40,48},{48,56},{56,64},{64,7... | collective-permute-start | bytes 294920 | tf_op jit(solution)/shard_map/while/body/eval_jaxpr/ppermute | solution.py:12
  520.5 9.8 %collective-permute-start.1 = (bf16[128,384]{0,1:T(8,128)(2,1)S(1)}, bf16[128,384]{0,1:T(8,128)(2,1)S(1)}, u32[]{:S(2)}, u32[]{:S(2)}) collective-permute-start(bf16[128,384]{0,1:T(8,128)(2,1)S(1)} %get-tuple-element.372), channel_id=1, source_target_pairs={{0,8},{8,16},{16,24},{24,32},{32,40},{40,48},{48,56},{56,64},{64,7... | collective-permute-start | bytes 294920 | tf_op jit(solution)/shard_map/while/body/eval_jaxpr/ppermute | solution.py:12
  542.7 9.8 %collective-permute-start = (bf16[128,384]{0,1:T(8,128)(2,1)S(1)}, bf16[128,384]{0,1:T(8,128)(2,1)S(1)}, u32[]{:S(2)}, u32[]{:S(2)}) collective-permute-start(bf16[128,384]{0,1:T(8,128)(2,1)S(1)} %get-tuple-element.371), channel_id=1, source_target_pairs={{0,8},{8,16},{16,24},{24,32},{32,40},{40,48},{48,56},{56,64},{64,7... | collective-permute-start | bytes 294920 | tf_op jit(solution)/shard_map/while/body/eval_jaxpr/ppermute | solution.py:12
  544.7 9.8 %collective-permute-start.1 = (bf16[128,384]{0,1:T(8,128)(2,1)S(1)}, bf16[128,384]{0,1:T(8,128)(2,1)S(1)}, u32[]{:S(2)}, u32[]{:S(2)}) collective-permute-start(bf16[128,384]{0,1:T(8,128)(2,1)S(1)} %get-tuple-element.372), channel_id=1, source_target_pairs={{0,8},{8,16},{16,24},{24,32},{32,40},{40,48},{48,56},{56,64},{64,7... | collective-permute-start | bytes 294920 | tf_op jit(solution)/shard_map/while/body/eval_jaxpr/ppermute | solution.py:12
  554.8 9.8 %collective-permute-start = (bf16[128,384]{0,1:T(8,128)(2,1)S(1)}, bf16[128,384]{0,1:T(8,128)(2,1)S(1)}, u32[]{:S(2)}, u32[]{:S(2)}) collective-permute-start(bf16[128,384]{0,1:T(8,128)(2,1)S(1)} %get-tuple-element.371), channel_id=1, source_target_pairs={{0,8},{8,16},{16,24},{24,32},{32,40},{40,48},{48,56},{56,64},{64,7... | collective-permute-start | bytes 294920 | tf_op jit(solution)/shard_map/while/body/eval_jaxpr/ppermute | solution.py:12
  556.7 9.8 %collective-permute-start.1 = (bf16[128,384]{0,1:T(8,128)(2,1)S(1)}, bf16[128,384]{0,1:T(8,128)(2,1)S(1)}, u32[]{:S(2)}, u32[]{:S(2)}) collective-permute-start(bf16[128,384]{0,1:T(8,128)(2,1)S(1)} %get-tuple-element.372), channel_id=1, source_target_pairs={{0,8},{8,16},{16,24},{24,32},{32,40},{40,48},{48,56},{56,64},{64,7... | collective-permute-start | bytes 294920 | tf_op jit(solution)/shard_map/while/body/eval_jaxpr/ppermute | solution.py:12
  579.0 9.8 %collective-permute-start = (bf16[128,384]{0,1:T(8,128)(2,1)S(1)}, bf16[128,384]{0,1:T(8,128)(2,1)S(1)}, u32[]{:S(2)}, u32[]{:S(2)}) collective-permute-start(bf16[128,384]{0,1:T(8,128)(2,1)S(1)} %get-tuple-element.371), channel_id=1, source_target_pairs={{0,8},{8,16},{16,24},{24,32},{32,40},{40,48},{48,56},{56,64},{64,7... | collective-permute-start | bytes 294920 | tf_op jit(solution)/shard_map/while/body/eval_jaxpr/ppermute | solution.py:12
  580.9 9.8 %collective-permute-start.1 = (bf16[128,384]{0,1:T(8,128)(2,1)S(1)}, bf16[128,384]{0,1:T(8,128)(2,1)S(1)}, u32[]{:S(2)}, u32[]{:S(2)}) collective-permute-start(bf16[128,384]{0,1:T(8,128)(2,1)S(1)} %get-tuple-element.372), channel_id=1, source_target_pairs={{0,8},{8,16},{16,24},{24,32},{32,40},{40,48},{48,56},{56,64},{64,7... | collective-permute-start | bytes 294920 | tf_op jit(solution)/shard_map/while/body/eval_jaxpr/ppermute | solution.py:12
  603.1 9.8 %collective-permute-start = (bf16[128,384]{0,1:T(8,128)(2,1)S(1)}, bf16[128,384]{0,1:T(8,128)(2,1)S(1)}, u32[]{:S(2)}, u32[]{:S(2)}) collective-permute-start(bf16[128,384]{0,1:T(8,128)(2,1)S(1)} %get-tuple-element.371), channel_id=1, source_target_pairs={{0,8},{8,16},{16,24},{24,32},{32,40},{40,48},{48,56},{56,64},{64,7... | collective-permute-start | bytes 294920 | tf_op jit(solution)/shard_map/while/body/eval_jaxpr/ppermute | solution.py:12
  605.1 9.8 %collective-permute-start.1 = (bf16[128,384]{0,1:T(8,128)(2,1)S(1)}, bf16[128,384]{0,1:T(8,128)(2,1)S(1)}, u32[]{:S(2)}, u32[]{:S(2)}) collective-permute-start(bf16[128,384]{0,1:T(8,128)(2,1)S(1)} %get-tuple-element.372), channel_id=1, source_target_pairs={{0,8},{8,16},{16,24},{24,32},{32,40},{40,48},{48,56},{56,64},{64,7... | collective-permute-start | bytes 294920 | tf_op jit(solution)/shard_map/while/body/eval_jaxpr/ppermute | solution.py:12
  615.2 9.8 %collective-permute-start = (bf16[128,384]{0,1:T(8,128)(2,1)S(1)}, bf16[128,384]{0,1:T(8,128)(2,1)S(1)}, u32[]{:S(2)}, u32[]{:S(2)}) collective-permute-start(bf16[128,384]{0,1:T(8,128)(2,1)S(1)} %get-tuple-element.371), channel_id=1, source_target_pairs={{0,8},{8,16},{16,24},{24,32},{32,40},{40,48},{48,56},{56,64},{64,7... | collective-permute-start | bytes 294920 | tf_op jit(solution)/shard_map/while/body/eval_jaxpr/ppermute | solution.py:12
  617.2 9.8 %collective-permute-start.1 = (bf16[128,384]{0,1:T(8,128)(2,1)S(1)}, bf16[128,384]{0,1:T(8,128)(2,1)S(1)}, u32[]{:S(2)}, u32[]{:S(2)}) collective-permute-start(bf16[128,384]{0,1:T(8,128)(2,1)S(1)} %get-tuple-element.372), channel_id=1, source_target_pairs={{0,8},{8,16},{16,24},{24,32},{32,40},{40,48},{48,56},{56,64},{64,7... | collective-permute-start | bytes 294920 | tf_op jit(solution)/shard_map/while/body/eval_jaxpr/ppermute | solution.py:12
  639.4 9.8 %collective-permute-start = (bf16[128,384]{0,1:T(8,128)(2,1)S(1)}, bf16[128,384]{0,1:T(8,128)(2,1)S(1)}, u32[]{:S(2)}, u32[]{:S(2)}) collective-permute-start(bf16[128,384]{0,1:T(8,128)(2,1)S(1)} %get-tuple-element.371), channel_id=1, source_target_pairs={{0,8},{8,16},{16,24},{24,32},{32,40},{40,48},{48,56},{56,64},{64,7... | collective-permute-start | bytes 294920 | tf_op jit(solution)/shard_map/while/body/eval_jaxpr/ppermute | solution.py:12
  724.0 9.9 %collective-permute-start = (bf16[128,384]{0,1:T(8,128)(2,1)S(1)}, bf16[128,384]{0,1:T(8,128)(2,1)S(1)}, u32[]{:S(2)}, u32[]{:S(2)}) collective-permute-start(bf16[128,384]{0,1:T(8,128)(2,1)S(1)} %get-tuple-element.371), channel_id=1, source_target_pairs={{0,8},{8,16},{16,24},{24,32},{32,40},{40,48},{48,56},{56,64},{64,7... | collective-permute-start | bytes 294920 | tf_op jit(solution)/shard_map/while/body/eval_jaxpr/ppermute | solution.py:12
  725.9 9.9 %collective-permute-start.1 = (bf16[128,384]{0,1:T(8,128)(2,1)S(1)}, bf16[128,384]{0,1:T(8,128)(2,1)S(1)}, u32[]{:S(2)}, u32[]{:S(2)}) collective-permute-start(bf16[128,384]{0,1:T(8,128)(2,1)S(1)} %get-tuple-element.372), channel_id=1, source_target_pairs={{0,8},{8,16},{16,24},{24,32},{32,40},{40,48},{48,56},{56,64},{64,7... | collective-permute-start | bytes 294920 | tf_op jit(solution)/shard_map/while/body/eval_jaxpr/ppermute | solution.py:12
  760.3 9.8 %collective-permute-start = (bf16[128,384]{0,1:T(8,128)(2,1)S(1)}, bf16[128,384]{0,1:T(8,128)(2,1)S(1)}, u32[]{:S(2)}, u32[]{:S(2)}) collective-permute-start(bf16[128,384]{0,1:T(8,128)(2,1)S(1)} %get-tuple-element.371), channel_id=1, source_target_pairs={{0,8},{8,16},{16,24},{24,32},{32,40},{40,48},{48,56},{56,64},{64,7... | collective-permute-start | bytes 294920 | tf_op jit(solution)/shard_map/while/body/eval_jaxpr/ppermute | solution.py:12
  784.5 9.8 %collective-permute-start = (bf16[128,384]{0,1:T(8,128)(2,1)S(1)}, bf16[128,384]{0,1:T(8,128)(2,1)S(1)}, u32[]{:S(2)}, u32[]{:S(2)}) collective-permute-start(bf16[128,384]{0,1:T(8,128)(2,1)S(1)} %get-tuple-element.371), channel_id=1, source_target_pairs={{0,8},{8,16},{16,24},{24,32},{32,40},{40,48},{48,56},{56,64},{64,7... | collective-permute-start | bytes 294920 | tf_op jit(solution)/shard_map/while/body/eval_jaxpr/ppermute | solution.py:12
  786.4 9.8 %collective-permute-start.1 = (bf16[128,384]{0,1:T(8,128)(2,1)S(1)}, bf16[128,384]{0,1:T(8,128)(2,1)S(1)}, u32[]{:S(2)}, u32[]{:S(2)}) collective-permute-start(bf16[128,384]{0,1:T(8,128)(2,1)S(1)} %get-tuple-element.372), channel_id=1, source_target_pairs={{0,8},{8,16},{16,24},{24,32},{32,40},{40,48},{48,56},{56,64},{64,7... | collective-permute-start | bytes 294920 | tf_op jit(solution)/shard_map/while/body/eval_jaxpr/ppermute | solution.py:12
  (68 other events, 642.2 us)
where the time goes:
time: 833 us; the launch traced here: 821 us
  waiting for transfers between devices  475 us (57%)
  starting transfers between devices  271 us (33%)
  matrix products  45.6 us (5%)
  blocking collectives  11.7 us (1%)
    ppermute x126, waiting for transfers between devices, shifted(): lax.ppermute(x, axis, [(i, (i + by) % length) for i in range(length)])  450 us
    ppermute x126, starting transfers between devices, shifted(): lax.ppermute(x, axis, [(i, (i + by) % length) for i in range(length)])  250 us
  transfers between devices with their start and end apart: 129, of which 128 were waited for; matrix products, arithmetic and copies ran while one was open for 4% of the time, Pallas kernels for 0%

commit v1 on v0

v1 whole, which is shorter than its diff:
```python
import jax
import jax.numpy as jnp
from jax import lax
from jax.experimental import pallas as pl
from jax.experimental.pallas import tpu as pltpu
from jax.sharding import PartitionSpec as P

MESH = pl.DeviceIdType.MESH
D = 128
HEADS = 24
NX, NYH, NZ = 4, 4, 8
ROWS = 16
SRC = NYH * NZ
GROUP = SRC * ROWS
QTILES = 16
SLOTS = 32
PART = 32
CHUNKS = 4
PER_CHUNK = QTILES // CHUNKS
SCALE = 1.4426950408889634 / 128**0.5
LOW = -1e30
F32, BF16 = jnp.float32, jnp.bfloat16


def kernel(
    q_hbm, k_hbm, v_hbm, list_ref, out_ref,
    qin, kvin, list_src, lists, used, places, places_s, kv, qs, part, got, stat, got_stat, fin,
    in_sem, self_sem, a_send, a_recv, kv_send, kv_recv, q_send, q_recv, d_send, d_recv, s_send, s_recv, e_sem, e_self,
):
    blk, uly = lax.axis_index("blk"), lax.axis_index("uly")
    c, y, zl = blk % 2, (blk // 2) % 8, blk // 16
    x, zh = uly // 2, uly % 2
    yh, yl = y // 2, y % 2
    z = zh * 4 + zl
    active = yh < 3

    def device(x, yh, yl, z, c):
        return (((z % 4) * 8 + yh * 2 + yl) * 2 + c, x * 2 + z // 4)

    def slot(yh, z):
        return ((z % 4) * 4 + yh) * 2 + z // 4

    loads = [
        pltpu.make_async_copy(k_hbm, kvin.at[0], in_sem.at[0]),
        pltpu.make_async_copy(v_hbm, kvin.at[1], in_sem.at[1]),
        pltpu.make_async_copy(q_hbm, qin, in_sem.at[2]),
    ]
    for load in loads:
        load.start()

    barrier = pltpu.get_barrier_semaphore()

    def greet(i, carry):
        tyh, tz = (yh + i // NZ) % NYH, (z + i) % NZ

        @pl.when(jnp.logical_or(active, tyh < 3))
        def _():
            pl.semaphore_signal(barrier, inc=1, device_id=device(x, tyh, yl, tz, c), device_id_type=MESH)

        return carry

    lax.fori_loop(1, SRC, greet, 0)
    chip_peer = device(x, yh, yl, z, 1 - c)
    y_peer = device(x, yh, 1 - yl, z, c)
    x_peers = [device((x + r) % NX, yh, yl, z, c) for r in range(1, NX)]

    @pl.when(active)
    def _():
        for peer in (chip_peer, y_peer, *x_peers):
            pl.semaphore_signal(barrier, inc=1, device_id=peer, device_id_type=MESH)

    list_src[...] = jnp.full_like(list_src, -1)
    list_src[:, 0:SLOTS] = list_ref[...]
    stat[...] = jnp.zeros_like(stat)

    @pl.when(active)
    def _():
        pl.semaphore_wait(barrier, SRC - 1 + 5)

    @pl.when(jnp.logical_not(active))
    def _():
        pl.semaphore_wait(barrier, HEADS)

    mine = slot(yh, z)
    own = yl * 2 + c

    def kv_cols(h):
        return kvin.at[:, :, pl.ds(pl.multiple_of(h * D, D), D)]

    def q_cols(h):
        return qin.at[:, pl.ds(pl.multiple_of(h * D, D), D)]

    kv_rows = kv.at[:, own * QTILES + mine // 2, pl.ds(pl.multiple_of(mine % 2 * ROWS, ROWS), ROWS), :]
    q_rows = qs.at[x, pl.ds(pl.multiple_of(mine * ROWS, ROWS), ROWS), :]
    list_row = lists.at[mine]

    def target(i):
        tyh, tz = (yh + i % 3) % 3, (z + i // 3) % NZ
        return tz * 3 + tyh, device(x, tyh, yl, tz, c)

    def send_kv(i, carry):
        h, dev = target(i)
        pltpu.make_async_remote_copy(kv_cols(h), kv_rows, a_send.at[0], a_recv.at[0], device_id=dev, device_id_type=MESH).start()
        return carry

    def send_q(i, carry):
        h, dev = target(i)
        pltpu.make_async_remote_copy(q_cols(h), q_rows, a_send.at[1], a_recv.at[1], device_id=dev, device_id_type=MESH).start()
        pltpu.make_async_remote_copy(list_src, list_row, a_send.at[2], a_recv.at[2], device_id=dev, device_id_type=MESH).start()
        return carry

    head = z * 3 + yh
    first = jnp.where(active, 1, 0)
    loads[0].wait()
    loads[1].wait()
    lax.fori_loop(first, HEADS, send_kv, 0)
    loads[2].wait()
    lax.fori_loop(first, HEADS, send_q, 0)

    @pl.when(active)
    def _():
        selves = [
            pltpu.make_async_copy(kv_cols(head), kv_rows, self_sem.at[0]),
            pltpu.make_async_copy(q_cols(head), q_rows, self_sem.at[1]),
            pltpu.make_async_copy(list_src, list_row, self_sem.at[2]),
        ]
        for copy in selves:
            copy.start()

        def kv_copy(i, which, place, dev):
            block = kv.at[which, pl.ds(place * QTILES, QTILES)]
            return pltpu.make_async_remote_copy(block, block, kv_send.at[i], kv_recv.at[i], device_id=dev, device_id_type=MESH)

        far = (1 - yl) * 2 + c
        y_copies = [kv_copy(w, w, own, y_peer) for w in range(2)]
        chip_copies = [kv_copy(2 + w, w, own, chip_peer) for w in range(2)]
        on_copies = [kv_copy(4 + w, w, far, chip_peer) for w in range(2)]
        q_copies = [
            pltpu.make_async_remote_copy(qs.at[x], qs.at[x], q_send.at[r], q_recv.at[r], device_id=x_peers[r], device_id_type=MESH)
            for r in range(NX - 1)
        ]
        n = (SRC - 1) * ROWS
        selves[0].wait()
        arrived = kv.at[0, pl.ds(0, SRC - 1)]
        pltpu.make_async_copy(arrived, arrived, a_recv.at[0]).wait()
        for copy in y_copies:
            copy.start()
        for copy in chip_copies:
            copy.start()
        selves[1].wait()
        arrived = qs.at[0, pl.ds(0, n), :]
        pltpu.make_async_copy(arrived, arrived, a_recv.at[1]).wait()
        for copy in q_copies:
            copy.start()
        selves[2].wait()
        arrived = lists.at[pl.ds(0, SRC - 1)]
        pltpu.make_async_copy(arrived, arrived, a_recv.at[2]).wait()
        listed = lists[...]
        used[...] = jnp.broadcast_to(jnp.sum(jnp.where(listed >= 0, PART, 0), axis=2, keepdims=True), used.shape)
        listed = jnp.maximum(listed, 0)
        places[...] = (listed & 3) * QTILES + (listed >> 2)
        to_scalars = pltpu.make_async_copy(places, places_s, self_sem.at[3])
        to_scalars.start()
        for w in range(2):
            y_copies[w].wait_recv()
            on_copies[w].start()
        to_scalars.wait()
        for copy in q_copies:
            copy.wait_recv()
        for copy in chip_copies + on_copies:
            copy.wait_recv()

        lane = lax.broadcasted_iota(jnp.int32, (D, D), 1)
        key_lane = lax.broadcasted_iota(jnp.int32, (1, 256), 1)
        ones = jnp.ones((256, D), BF16)

        def tile(t):
            query = jnp.concatenate([qs[i, pl.ds(pl.multiple_of(t * PART, PART), PART), :] for i in range(NX)], axis=0)
            blocks = [places_s[2 * t, 0, s] for s in range(SLOTS)]
            limit = used[2 * t]
            limit = jnp.concatenate([limit, limit], axis=1)
            scores = []
            for g in range(4):
                keys = jnp.concatenate([kv[0, b] for b in blocks[g * 8 : g * 8 + 8]], axis=0)
                s = lax.dot_general(query, keys, (((1,), (1,)), ((), ())), preferred_element_type=F32)
                scores.append(s + jnp.where(key_lane < limit - g * 256, 0.0, LOW))
            top = jnp.maximum(jnp.maximum(scores[0], scores[1]), jnp.maximum(scores[2], scores[3]))
            top = jnp.max(top, axis=1, keepdims=True)
            total = jnp.zeros((D, 2 * D), F32)
            for g in range(4):
                weights = jnp.exp2((scores[g] - top) * SCALE).astype(BF16)
                values = jnp.concatenate([kv[1, b] for b in blocks[g * 8 : g * 8 + 8]], axis=0)
                total = total + jnp.dot(weights, jnp.concatenate([values, ones], axis=1), preferred_element_type=F32)
            stat[...] = jnp.where(lane == t, top, jnp.where(lane == t + 64, total[:, D:], stat[...]))
            numerator = total[:, :D].astype(BF16)
            for i in range(NX):
                part[(i - x + NX) % NX, pl.ds(pl.multiple_of(t * PART, PART), PART), :] = numerator[i * PART : (i + 1) * PART]

        def part_copy(k, r):
            rows = pl.ds(pl.multiple_of(k * (PER_CHUNK * PART), PER_CHUNK * PART), PER_CHUNK * PART)
            return pltpu.make_async_remote_copy(
                part.at[r, rows, :], got.at[r - 1, rows, :], d_send.at[k, r - 1], d_recv.at[k, r - 1],
                device_id=x_peers[r - 1], device_id_type=MESH,
            )

        def chunk(k, carry):
            lax.fori_loop(0, PER_CHUNK, lambda i, n: (tile(k * PER_CHUNK + i), n)[1], 0)
            for r in range(1, NX):
                part_copy(k, r).start()
            return carry

        lax.fori_loop(0, CHUNKS, chunk, 0)
        stat_copies = [
            pltpu.make_async_remote_copy(
                stat.at[pl.ds(pl.multiple_of(((x + r) % NX) * PART, PART), PART), :], got_stat.at[r - 1],
                s_send.at[r - 1], s_recv.at[r - 1], device_id=x_peers[r - 1], device_id_type=MESH,
            )
            for r in range(1, NX)
        ]
        for copy in stat_copies:
            copy.start()

        for copy in stat_copies:
            copy.wait_recv()
        stats = [stat[pl.ds(pl.multiple_of(x * PART, PART), PART), :]] + [got_stat[r] for r in range(NX - 1)]
        highest = jnp.maximum(jnp.maximum(stats[0], stats[1]), jnp.maximum(stats[2], stats[3]))
        factors = [jnp.exp2((s - highest) * SCALE) for s in stats]
        denominator = sum(f[:, 0:QTILES] * s[:, 64 : 64 + QTILES] for f, s in zip(factors, stats))
        factors = [f[:, 0:QTILES] / denominator for f in factors]
        for k in range(CHUNKS):
            for r in range(1, NX):
                part_copy(k, r).wait_recv()
            for t in range(k * PER_CHUNK, (k + 1) * PER_CHUNK):
                rows = slice(t * PART, (t + 1) * PART)
                terms = [part[0, rows, :]] + [got[r, rows, :] for r in range(NX - 1)]
                fin[rows, :] = sum(f[:, t : t + 1] * a.astype(F32) for f, a in zip(factors, terms)).astype(BF16)

        columns = out_ref.at[:, pl.ds(pl.multiple_of(head * D, D), D)]

        def fin_rows(s):
            return fin.at[pl.ds(pl.multiple_of(s * ROWS, ROWS), ROWS), :]

        def send_out(i, carry):
            tyh, tz = (yh + i // NZ) % NYH, (z + i) % NZ
            dev = device(x, tyh, yl, tz, c)
            pltpu.make_async_remote_copy(
                fin_rows(slot(tyh, tz)), columns, e_sem.at[0], e_sem.at[1], device_id=dev, device_id_type=MESH
            ).start()
            return carry

        lax.fori_loop(1, SRC, send_out, 0)
        last = pltpu.make_async_copy(fin_rows(mine), columns, e_self)
        last.start()

        for copy in y_copies + chip_copies + on_copies + q_copies + stat_copies:
            copy.wait_send()
        for k in range(CHUNKS):
            for r in range(1, NX):
                part_copy(k, r).wait_send()
        last.wait()
        sent = fin.at[pl.ds(0, n), :]
        pltpu.make_async_copy(sent, sent, e_sem.at[0]).wait()

    def finish(count):
        cols = pl.ds(0, count * D)
        for ref, sem in (
            (kvin.at[:, :, cols], a_send.at[0]),
            (qin.at[:, cols], a_send.at[1]),
            (lists.at[pl.ds(0, count)], a_send.at[2]),
            (out_ref.at[:, cols], e_sem.at[1]),
        ):
            pltpu.make_async_copy(ref, ref, sem).wait()

    @pl.when(active)
    def _():
        finish(HEADS - 1)

    @pl.when(jnp.logical_not(active))
    def _():
        finish(HEADS)


def per_device(query, key, value, tile_list):
    dma = pltpu.SemaphoreType.DMA
    return pl.pallas_call(
        kernel,
        out_shape=jax.ShapeDtypeStruct(query.shape, BF16),
        in_specs=[pl.BlockSpec(memory_space=pl.ANY)] * 3 + [pl.BlockSpec(memory_space=pltpu.VMEM)],
        out_specs=pl.BlockSpec(memory_space=pl.ANY),
        scratch_shapes=[
            pltpu.VMEM((ROWS, HEADS * D), BF16),
            pltpu.VMEM((2, ROWS, HEADS * D), BF16),
            pltpu.VMEM((1, D), jnp.int32),
            pltpu.VMEM((SRC, 1, D), jnp.int32),
            pltpu.VMEM((SRC, 1, D), jnp.int32),
            pltpu.VMEM((SRC, 1, D), jnp.int32),
            pltpu.SMEM((SRC, 1, D), jnp.int32),
            pltpu.VMEM((2, 4 * QTILES, PART, D), BF16),
            pltpu.VMEM((NX, GROUP, D), BF16),
            pltpu.VMEM((NX, GROUP, D), BF16),
            pltpu.VMEM((NX - 1, GROUP, D), BF16),
            pltpu.VMEM((D, D), F32),
            pltpu.VMEM((NX - 1, PART, D), F32),
            pltpu.VMEM((GROUP, D), BF16),
            dma((3,)), dma((4,)), dma((3,)), dma((3,)), dma((6,)), dma((6,)), dma((3,)), dma((3,)),
            dma((CHUNKS, 3)), dma((CHUNKS, 3)), dma((3,)), dma((3,)), dma((2,)), dma,
        ],
        compiler_params=pltpu.CompilerParams(
            collective_id=0, has_side_effects=True, vmem_limit_bytes=32 * 1024 * 1024
        ),
        name="attention",
    )(query, key, value, tile_list)


def solution(mesh):
    rows = P(("blk", "uly"), None)
    return jax.shard_map(
        per_device,
        mesh=mesh,
        in_specs=(rows, rows, rows, P("blk", None)),
        out_specs=rows,
        check_vma=False,
    )
```

time: 833 us -> 63.3 us (0.08); the launches traced: 821 us -> 63.1 us
  waiting for transfers between devices: 475 us -> 0 us
  starting transfers between devices: 271 us -> 0 us
  Pallas kernels: 0 us -> 59.1 us
  matrix products: 45.6 us -> 0 us
  blocking collectives: 11.7 us -> 0 us
    ppermute x126 -> x0, waiting for transfers between devices: 450 us -> none  [shifted(): lax.ppermute(x, axis, [(i, (i + by) % length) for i in range(length)])]
    ppermute x126 -> x0, starting transfers between devices: 250 us -> none  [shifted(): lax.ppermute(x, axis, [(i, (i + by) % length) for i in range(length)])]
    pallas_call x0 -> x1, Pallas kernels: none -> 59.1 us  [per_device(): pl.pallas_call(kernel, out_shape=jax.ShapeDtypeStruct(query.shape, BF16),...]
    dot_general x192 -> x0, matrix products: 45.6 us -> none  [the longest x64 16.5 us: attend(): jnp.einsum('hqk,khd->qhd', weights, values_3d, preferred_element_type=jnp...]
    all_to_all x3 -> x0, waiting for transfers between devices: 24.9 us -> none  [the longest x1 9.18 us: per_device(): lax.all_to_all(key, 'uly', split_axis=1, concat_axis=0, tiled=True)]
    all_to_all x3 -> x0, starting transfers between devices: 20.1 us -> none  [the longest x1 13.4 us: per_device(): lax.all_to_all(query, 'uly', split_axis=1, concat_axis=0, tiled=True)]
    all_to_all x1 -> x0, blocking collectives: 11.7 us -> none  [per_device(): lax.all_to_all(result, 'uly', split_axis=0, concat_axis=1, tiled=True)]
  transfers between devices with their start and end apart: 129 -> 0, of which waited for: 128 -> 0; matrix products, arithmetic and copies ran while one was open for 4% -> 0% of each run, Pallas kernels for 0% -> 0%
where the time goes in v1:
time: 63.3 us; the launch traced here: 63.1 us
  Pallas kernels  59.1 us (93%)
  local copies, waits for them, and re-layouts  3.97 us (6%)
    pallas_call x1, Pallas kernels, per_device(): pl.pallas_call(kernel, out_shape=jax.ShapeDtypeStruct(query.shape, BF16),...  59.1 us
    unnamed x9, local copies, waits for them, and re-layouts  3.97 us

profile of v1, /device:TPU:1, one launch (start us, length us, event | category | flops | bytes accessed | tf_op | source)
XLA Modules:
  0.0 63.1 jit_solution(7267758019327512189)
XLA Ops:
  0.0 0.0 copy-start
  0.0 0.9 %copy-done = bf16[16,3072]{1,0:T(8,128)(2,1)S(1)} copy-done((bf16[16,3072]{1,0:T(8,128)(2,1)S(1)}, bf16[16,3072]{1,0:T(8,128)(2,1)}, u32[]{:S(2)}) %copy-start) | copy-done | bytes 98328
  0.9 0.0 copy-start.1
  0.9 0.9 %copy-done.1 = bf16[16,3072]{1,0:T(8,128)(2,1)S(1)} copy-done((bf16[16,3072]{1,0:T(8,128)(2,1)S(1)}, bf16[16,3072]{1,0:T(8,128)(2,1)}, u32[]{:S(2)}) %copy-start.1) | copy-done | bytes 98328
  1.8 0.0 copy-start.2
  1.8 0.9 %copy-done.2 = bf16[16,3072]{1,0:T(8,128)(2,1)S(1)} copy-done((bf16[16,3072]{1,0:T(8,128)(2,1)S(1)}, bf16[16,3072]{1,0:T(8,128)(2,1)}, u32[]{:S(2)}) %copy-start.2) | copy-done | bytes 98328
  2.7 0.0 copy-start.3
  2.7 0.7 %copy-done.3 = s32[1,32]{1,0:T(1,128)S(1)} copy-done((s32[1,32]{1,0:T(1,128)S(1)}, s32[1,32]{1,0:T(1,128)}, u32[]{:S(2)}) %copy-start.3) | copy-done | bytes 152
  3.3 59.1 %attention.1 = bf16[16,3072]{1,0:T(8,128)(2,1)S(1)} custom-call(bf16[16,3072]{1,0:T(8,128)(2,1)S(1)} %copy-done, bf16[16,3072]{1,0:T(8,128)(2,1)S(1)} %copy-done.1, bf16[16,3072]{1,0:T(8,128)(2,1)S(1)} %copy-done.2, s32[1,32]{1,0:T(1,128)S(1)} %copy-done.3), custom_call_target="tpu_custom_call" | custom-call | tf_op jit(solution)/shard_map/attention/pallas_call | solution.py:285
  62.4 0.6 %copy.6 = bf16[16,3072]{1,0:T(8,128)(2,1)} copy(bf16[16,3072]{1,0:T(8,128)(2,1)S(1)} %attention.1) | data formatting | bytes 196608
Async XLA Ops:
  0.0 0.9 %copy-start = (bf16[16,3072]{1,0:T(8,128)(2,1)S(1)}, bf16[16,3072]{1,0:T(8,128)(2,1)}, u32[]{:S(2)}) copy-start(bf16[16,3072]{1,0:T(8,128)(2,1)} %q_hbm.1) | copy-start | bytes 294916
  0.9 0.9 %copy-start.1 = (bf16[16,3072]{1,0:T(8,128)(2,1)S(1)}, bf16[16,3072]{1,0:T(8,128)(2,1)}, u32[]{:S(2)}) copy-start(bf16[16,3072]{1,0:T(8,128)(2,1)} %k_hbm.1) | copy-start | bytes 294916
  1.8 0.9 %copy-start.2 = (bf16[16,3072]{1,0:T(8,128)(2,1)S(1)}, bf16[16,3072]{1,0:T(8,128)(2,1)}, u32[]{:S(2)}) copy-start(bf16[16,3072]{1,0:T(8,128)(2,1)} %v_hbm.1) | copy-start | bytes 294916
  2.7 0.7 %copy-start.3 = (s32[1,32]{1,0:T(1,128)S(1)}, s32[1,32]{1,0:T(1,128)}, u32[]{:S(2)}) copy-start(s32[1,32]{1,0:T(1,128)} %list_ref.1) | copy-start | bytes 388

commit v2 on v0

v2 whole, which is shorter than its diff:
```python
import jax
import jax.numpy as jnp
from jax import lax
from jax.experimental import pallas as pl
from jax.experimental.pallas import tpu as pltpu
from jax.sharding import PartitionSpec as P

MESH = pl.DeviceIdType.MESH
D = 128
HEADS = 24
ROWS = 16
SRC = 32
TILES = 16
HALF = TILES
SLOTS = 32
PART = 32
CHUNKS = 8
PER_CHUNK = 2
SCALE = 1.4426950408889634 / 128**0.5
LOW = -1e30
F32, BF16 = jnp.float32, jnp.bfloat16


def kernel(
    q_hbm, k_hbm, v_hbm, list_ref, out_ref,
    list_src, list_room, lists, used, places, places_s, qkv, part, got, stat, got_stat, fin,
    list_sem, a_send, a_recv, b_send, b_recv, d_send, d_recv, s_send, s_recv, e_sem,
):
    blk, uly = lax.axis_index("blk"), lax.axis_index("uly")
    c, y, x = blk % 2, (blk // 2) % 8, uly // 2
    z = uly % 2 * 4 + blk // 16
    xh, xl, yh, yl, zc, zr = x // 2, x % 2, y // 2, y % 2, z // 2, z % 2
    active = zc < 3

    def device(x, y, z):
        return (((z % 4) * 8 + y) * 2 + c, x * 2 + z // 4)

    def turned(other):
        return jnp.where((other - yh) % 2 == 0, 1 - yl, yl)

    def crossed(other):
        return jnp.where(other == xh, xl, 1 - xl)

    def target(h):
        txh, tyh, tzc = h // 4 % 2, h % 4, h // 8
        zh = z // 4
        return device(2 * txh + crossed(txh), 2 * tyh + turned(tyh), 2 * tzc + jnp.where(tzc == 0, 1 - zh, zh))

    from_z = 4 * jnp.where(zc == 0, 1 - zr, zr)

    def source(s):
        sxh, syh = s // 16, s // 4 % 4
        return device(2 * sxh + crossed(sxh), 2 * syh + turned(syh), from_z + s % 4)

    head = zc * 8 + xh * 4 + yh
    tile = yh * 4 + z % 4
    mine = xh * HALF + tile

    rows_in = (q_hbm, k_hbm, v_hbm)

    def flip(value, by):
        return 1 - value if by else value

    chip_peer = (blk + 1 - 2 * c, uly)
    y_peer = device(x, 2 * yh + 1 - yl, z)
    q_peers = [device(2 * xh + flip(xl, r // 2), y, 2 * zc + flip(zr, r % 2)) for r in range(1, 4)]

    barrier = pltpu.get_barrier_semaphore()

    def greet(dev):
        pl.semaphore_signal(barrier, inc=1, device_id=dev, device_id_type=MESH)

    def loop(low, high, body):
        def step(i, carry):
            body(i)
            return carry

        lax.fori_loop(low, high, step, 0)

    @pl.when(active)
    def _():
        for peer in (chip_peer, y_peer, *q_peers):
            greet(peer)
        loop(0, SRC, lambda s: greet(source(s)))

    list_src[...] = jnp.full_like(list_src, -1)
    list_src[:, 0:SLOTS] = list_ref[...]
    stat[...] = jnp.zeros_like(stat)

    def spread(i, zcs):
        return (zc + i // 8) % zcs * 8 + (xh + i // 4) % 2 * 4 + (yh + i) % 4

    def send(which, h):
        pltpu.make_async_remote_copy(
            rows_in[which].at[:, pl.ds(pl.multiple_of(h * D, D), D)], qkv.at[which, mine], a_send.at[which], a_recv.at[which],
            device_id=target(h), device_id_type=MESH,
        ).start()

    def send_list(h):
        pltpu.make_async_remote_copy(
            list_src, lists.at[tile], a_send.at[3], a_recv.at[3], device_id=target(h), device_id_type=MESH
        ).start()

    @pl.when(active)
    def _():
        pl.semaphore_wait(barrier, HEADS + 5)

    @pl.when(jnp.logical_not(active))
    def _():
        pl.semaphore_wait(barrier, HEADS)

    @pl.when(xh == 0)
    def _():
        loop(0, HEADS, lambda i: send_list(spread(i, 3)))

    for which in range(3):
        loop(0, HEADS, lambda i: send(which, spread(i, 3)))

    def wait_for(ref, sem):
        pltpu.make_async_copy(ref, ref, sem).wait()

    @pl.when(active)
    def _():
        def block(which, place):
            return qkv.at[which, pl.ds(place * SRC, SRC)]

        def swap(which, src, dst, i, dev):
            return pltpu.make_async_remote_copy(
                block(which, src), block(which, dst), b_send.at[which, i], b_recv.at[which, i], device_id=dev, device_id_type=MESH
            )

        q_copies = [swap(0, 0, r, r - 1, q_peers[r - 1]) for r in range(1, 4)]
        y_copies = [None] + [swap(which, 0, 2, 0, y_peer) for which in (1, 2)]
        chip_copies = [None] + [swap(which, 0, 1, 1, chip_peer) for which in (1, 2)]
        on_copies = [None] + [swap(which, 2, 3, 2, chip_peer) for which in (1, 2)]

        wait_for(block(0, 0), a_recv.at[0])
        for copy in q_copies:
            copy.start()

        wait_for(lists, a_recv.at[3])
        listed = lists[...]
        used[...] = jnp.broadcast_to(jnp.sum(jnp.where(listed >= 0, 1, 0), axis=2, keepdims=True), used.shape)
        listed = jnp.maximum(listed, 0)
        tile_yh = (listed >> 2) & 3
        tile_yl = ((listed >> 1) & 1) ^ jnp.where((tile_yh - yh) % 2 == 0, 1, 0)
        place = (tile_yl ^ yl) * 2 + ((listed & 1) ^ c)
        places[...] = place * SRC + tile_yh * 4 + (listed >> 4)
        to_scalars = pltpu.make_async_copy(places, places_s, list_sem)
        to_scalars.start()

        for which in (1, 2):
            wait_for(block(which, 0), a_recv.at[which])
            y_copies[which].start()
            chip_copies[which].start()
        y_copies[1].wait_recv()
        on_copies[1].start()
        to_scalars.wait()
        for copy in q_copies + [chip_copies[1], on_copies[1]]:
            copy.wait_recv()

        y_copies[2].wait_recv()
        on_copies[2].start()
        for copy in (chip_copies[2], on_copies[2]):
            copy.wait_recv()

        lane = lax.broadcasted_iota(jnp.int32, (D, D), 1)
        key_slot = lax.broadcasted_iota(jnp.int32, (1, 256), 1) % D // ROWS
        ones = jnp.ones((256, D), BF16)

        def tiles(ts):
            blocks = [[places_s[t, 0, s] for s in range(SLOTS)] for t in ts]
            limits = [jnp.concatenate([used[t], used[t]], axis=1) for t in ts]

            def gathered(which, blocks, g):
                return jnp.concatenate(
                    [qkv[which, b + half * HALF] for half in range(2) for b in blocks[g * 8 : g * 8 + 8]], axis=0
                )

            scores = []
            for t, b, limit in zip(ts, blocks, limits):
                query = jnp.concatenate([qkv[0, r * SRC + half * HALF + t] for r in range(4) for half in range(2)], axis=0)
                scores.append([
                    lax.dot_general(query, gathered(1, b, g), (((1,), (1,)), ((), ())), preferred_element_type=F32)
                    + jnp.where(key_slot + g * 8 < limit, 0.0, LOW)
                    for g in range(4)
                ])
            tops = []
            for s in scores:
                top = jnp.maximum(jnp.maximum(s[0], s[1]), jnp.maximum(s[2], s[3]))
                tops.append(jnp.max(top, axis=1, keepdims=True))
            totals = []
            for b, s, top in zip(blocks, scores, tops):
                total = jnp.zeros((D, 2 * D), F32)
                for g in range(4):
                    weights = jnp.exp2((s[g] - top) * SCALE).astype(BF16)
                    values = jnp.concatenate([gathered(2, b, g), ones], axis=1)
                    total = total + jnp.dot(weights, values, preferred_element_type=F32)
                totals.append(total)
            stats = stat[...]
            for t, top, total in zip(ts, tops, totals):
                stats = jnp.where(lane == t, top, jnp.where(lane == t + 64, total[:, D:], stats))
                numerator = total[:, :D].astype(BF16)
                for r in range(4):
                    for half in range(2):
                        low = r * PART + half * ROWS
                        part[r, half, t] = numerator[low : low + ROWS]
            stat[...] = stats

        def part_copy(k, r):
            rows = pl.ds(k * PER_CHUNK, PER_CHUNK)
            return pltpu.make_async_remote_copy(
                part.at[r, :, rows], got.at[r - 1, :, rows], d_send.at[k, r - 1], d_recv.at[k, r - 1],
                device_id=q_peers[r - 1], device_id_type=MESH,
            )

        def chunk(k):
            loop(0, PER_CHUNK // 2, lambda i: tiles([k * PER_CHUNK + 2 * i, k * PER_CHUNK + 2 * i + 1]))
            for r in range(1, 4):
                part_copy(k, r).start()

        loop(0, CHUNKS, chunk)
        stat_copies = [
            pltpu.make_async_remote_copy(
                stat.at[pl.ds(r * PART, PART), :], got_stat.at[r - 1], s_send.at[r - 1], s_recv.at[r - 1],
                device_id=q_peers[r - 1], device_id_type=MESH,
            )
            for r in range(1, 4)
        ]
        for copy in stat_copies:
            copy.start()

        for copy in stat_copies:
            copy.wait_recv()
        stats = [stat[0:PART, :]] + [got_stat[r] for r in range(3)]
        highest = jnp.maximum(jnp.maximum(stats[0], stats[1]), jnp.maximum(stats[2], stats[3]))
        factors = [jnp.exp2((s - highest) * SCALE) for s in stats]
        denominator = sum(f[:, 0:TILES] * s[:, 64 : 64 + TILES] for f, s in zip(factors, stats))
        factors = [f[:, 0:TILES] / denominator for f in factors]
        for k in range(CHUNKS):
            for r in range(1, 4):
                part_copy(k, r).wait_recv()
            for t in range(k * PER_CHUNK, (k + 1) * PER_CHUNK):
                for half in range(2):
                    rows = slice(half * ROWS, (half + 1) * ROWS)
                    terms = [part[0, half, t]] + [got[r, half, t] for r in range(3)]
                    fin[half * HALF + t] = sum(f[rows, t : t + 1] * a.astype(F32) for f, a in zip(factors, terms)).astype(BF16)

        columns = out_ref.at[:, pl.ds(pl.multiple_of(head * D, D), D)]

        def send_out(i):
            s = (xh + i // 16) % 2 * HALF + (yh + i // 4) % 4 * 4 + (z + i) % 4
            pltpu.make_async_remote_copy(
                fin.at[s], columns, e_sem.at[0], e_sem.at[1], device_id=source(s), device_id_type=MESH
            ).start()

        loop(0, SRC, send_out)

        for copy in q_copies + y_copies[1:] + chip_copies[1:] + on_copies[1:] + stat_copies:
            copy.wait_send()
        for k in range(CHUNKS):
            for r in range(1, 4):
                part_copy(k, r).wait_send()
        wait_for(fin, e_sem.at[0])

    for which in range(3):
        wait_for(rows_in[which], a_send.at[which])
    wait_for(out_ref, e_sem.at[1])

    @pl.when(xh == 0)
    def _():
        wait_for(list_room, a_send.at[3])


def per_device(query, key, value, tile_list):
    dma = pltpu.SemaphoreType.DMA
    return pl.pallas_call(
        kernel,
        out_shape=jax.ShapeDtypeStruct(query.shape, BF16),
        in_specs=[pl.BlockSpec(memory_space=pltpu.HBM)] * 3 + [pl.BlockSpec(memory_space=pltpu.VMEM)],
        out_specs=pl.BlockSpec(memory_space=pl.ANY),
        scratch_shapes=[
            pltpu.VMEM((1, D), jnp.int32),
            pltpu.VMEM((HEADS, 1, D), jnp.int32),
            pltpu.VMEM((TILES, 1, D), jnp.int32),
            pltpu.VMEM((TILES, 1, D), jnp.int32),
            pltpu.VMEM((TILES, 1, D), jnp.int32),
            pltpu.SMEM((TILES, 1, D), jnp.int32),
            pltpu.VMEM((3, 4 * SRC, ROWS, D), BF16),
            pltpu.VMEM((4, 2, TILES, ROWS, D), BF16),
            pltpu.VMEM((3, 2, TILES, ROWS, D), BF16),
            pltpu.VMEM((D, D), F32),
            pltpu.VMEM((3, PART, D), F32),
            pltpu.VMEM((SRC, ROWS, D), BF16),
            dma, dma((4,)), dma((4,)), dma((3, 3)), dma((3, 3)),
            dma((CHUNKS, 3)), dma((CHUNKS, 3)), dma((3,)), dma((3,)), dma((2,)),
        ],
        compiler_params=pltpu.CompilerParams(
            collective_id=0, has_side_effects=True, vmem_limit_bytes=56 * 1024 * 1024
        ),
        name="attention",
    )(query, key, value, tile_list)


def solution(mesh):
    rows = P(("blk", "uly"), None)
    return jax.shard_map(
        per_device,
        mesh=mesh,
        in_specs=(rows, rows, rows, P("blk", None)),
        out_specs=rows,
        check_vma=False,
    )
```

time: 833 us -> 58.1 us (0.07); the launches traced: 821 us -> 58 us
  waiting for transfers between devices: 475 us -> 0 us
  starting transfers between devices: 271 us -> 0 us
  Pallas kernels: 0 us -> 56.4 us
  matrix products: 45.6 us -> 0 us
  blocking collectives: 11.7 us -> 0 us
    ppermute x126 -> x0, waiting for transfers between devices: 450 us -> none  [shifted(): lax.ppermute(x, axis, [(i, (i + by) % length) for i in range(length)])]
    ppermute x126 -> x0, starting transfers between devices: 250 us -> none  [shifted(): lax.ppermute(x, axis, [(i, (i + by) % length) for i in range(length)])]
    pallas_call x0 -> x1, Pallas kernels: none -> 56.4 us  [per_device(): pl.pallas_call(kernel, out_shape=jax.ShapeDtypeStruct(query.shape, BF16),...]
    dot_general x192 -> x0, matrix products: 45.6 us -> none  [the longest x64 16.5 us: attend(): jnp.einsum('hqk,khd->qhd', weights, values_3d, preferred_element_type=jnp...]
    all_to_all x3 -> x0, waiting for transfers between devices: 24.9 us -> none  [the longest x1 9.18 us: per_device(): lax.all_to_all(key, 'uly', split_axis=1, concat_axis=0, tiled=True)]
    all_to_all x3 -> x0, starting transfers between devices: 20.1 us -> none  [the longest x1 13.4 us: per_device(): lax.all_to_all(query, 'uly', split_axis=1, concat_axis=0, tiled=True)]
    all_to_all x1 -> x0, blocking collectives: 11.7 us -> none  [per_device(): lax.all_to_all(result, 'uly', split_axis=0, concat_axis=1, tiled=True)]
  transfers between devices with their start and end apart: 129 -> 0, of which waited for: 128 -> 0; matrix products, arithmetic and copies ran while one was open for 4% -> 0% of each run, Pallas kernels for 0% -> 0%
where the time goes in v2:
time: 58.1 us; the launch traced here: 58 us
  Pallas kernels  56.4 us (97%)
  local copies, waits for them, and re-layouts  1.54 us (3%)
    pallas_call x1, Pallas kernels, per_device(): pl.pallas_call(kernel, out_shape=jax.ShapeDtypeStruct(query.shape, BF16),...  56.4 us
    unnamed x1, local copies, waits for them, and re-layouts  1.54 us

profile of v2, /device:TPU:1, one launch (start us, length us, event | category | flops | bytes accessed | tf_op | source)
XLA Modules:
  0.0 58.0 jit_solution(17099549719547951666)
XLA Ops:
  0.0 56.4 %attention.1 = bf16[16,3072]{1,0:T(8,128)(2,1)} custom-call(bf16[16,3072]{1,0:T(8,128)(2,1)} %q_hbm.1, bf16[16,3072]{1,0:T(8,128)(2,1)} %k_hbm.1, bf16[16,3072]{1,0:T(8,128)(2,1)} %v_hbm.1, s32[1,32]{1,0:T(1,128)} %list_ref.1), custom_call_target="tpu_custom_call" | custom-call | tf_op jit(solution)/shard_map/attention/pallas_call | solution.py:277
  56.4 1.5 %copy.6 = bf16[16,3072]{1,0:T(8,128)(2,1)} copy(bf16[16,3072]{1,0:T(8,128)(2,1)} %attention.1) | data formatting | bytes 196608

commit v3 on v2

v3 whole, which is shorter than its diff:
```python
import jax
import jax.numpy as jnp
from jax import lax
from jax.experimental import pallas as pl
from jax.experimental.pallas import tpu as pltpu
from jax.sharding import PartitionSpec as P

MESH = pl.DeviceIdType.MESH
D = 128
HEADS = 24
ROWS = 16
SRC = 32
TILES = 16
HALF = TILES
SLOTS = 32
PART = 32
CHUNKS = 8
EARLY = 4
PER_CHUNK = 2
SCALE = 1.4426950408889634 / 128**0.5
LOW = -1e30
F32, BF16 = jnp.float32, jnp.bfloat16


def kernel(
    q_hbm, k_hbm, v_hbm, list_ref, out_ref,
    list_src, list_room, lists, used, places, places_s, q_rows, k_rows, v_rows, kept, part, got, stat, got_stat, fin,
    list_sem, a_send, a_recv, b_send, b_recv, d_send, d_recv, s_send, s_recv, e_sem,
):
    blk, uly = lax.axis_index("blk"), lax.axis_index("uly")
    c, y, x = blk % 2, (blk // 2) % 8, uly // 2
    z = uly % 2 * 4 + blk // 16
    xh, xl, yh, yl, zc, zr = x // 2, x % 2, y // 2, y % 2, z // 2, z % 2
    active = zc < 3

    def device(x, y, z):
        return (((z % 4) * 8 + y) * 2 + c, x * 2 + z // 4)

    def turned(other):
        return jnp.where((other - yh) % 2 == 0, 1 - yl, yl)

    def crossed(other):
        return jnp.where(other == xh, xl, 1 - xl)

    def target(h):
        txh, tyh, tzc = h // 4 % 2, h % 4, h // 8
        zh = z // 4
        return device(2 * txh + crossed(txh), 2 * tyh + turned(tyh), 2 * tzc + jnp.where(tzc == 0, 1 - zh, zh))

    from_z = 4 * jnp.where(zc == 0, 1 - zr, zr)

    def source(s):
        sxh, syh = s // 16, s // 4 % 4
        return device(2 * sxh + crossed(sxh), 2 * syh + turned(syh), from_z + s % 4)

    head = zc * 8 + xh * 4 + yh
    tile = yh * 4 + z % 4
    mine = xh * HALF + tile

    rows_in = (q_hbm, k_hbm, v_hbm)
    held = (q_rows, k_rows, v_rows)

    def flip(value, by):
        return 1 - value if by else value

    chip_peer = (blk + 1 - 2 * c, uly)
    y_peer = device(x, 2 * yh + 1 - yl, z)
    q_peers = [device(2 * xh + flip(xl, r // 2), y, 2 * zc + flip(zr, r % 2)) for r in range(1, 4)]

    barrier = pltpu.get_barrier_semaphore()

    def greet(dev):
        pl.semaphore_signal(barrier, inc=1, device_id=dev, device_id_type=MESH)

    def loop(low, high, body):
        def step(i, carry):
            body(i)
            return carry

        lax.fori_loop(low, high, step, 0)

    @pl.when(active)
    def _():
        for peer in (chip_peer, y_peer, *q_peers):
            greet(peer)
        loop(0, SRC, lambda s: greet(source(s)))

    list_src[...] = jnp.full_like(list_src, -1)
    list_src[:, 0:SLOTS] = list_ref[...]
    stat[...] = jnp.zeros_like(stat)

    def spread(i, zcs):
        return (jnp.where(zc < 2, 2, 0) + i // 8) % zcs * 8 + (xh + 1 + i // 4) % 2 * 4 + (yh + 2 + i) % 4

    def send(which, h):
        pltpu.make_async_remote_copy(
            rows_in[which].at[:, pl.ds(pl.multiple_of(h * D, D), D)], held[which].at[mine], a_send.at[which], a_recv.at[which],
            device_id=target(h), device_id_type=MESH,
        ).start()

    def send_list(h):
        pltpu.make_async_remote_copy(
            list_src, lists.at[tile], a_send.at[3], a_recv.at[3], device_id=target(h), device_id_type=MESH
        ).start()

    @pl.when(active)
    def _():
        pl.semaphore_wait(barrier, HEADS + 5)

    @pl.when(jnp.logical_not(active))
    def _():
        pl.semaphore_wait(barrier, HEADS)

    @pl.when(xh == 0)
    def _():
        loop(0, HEADS, lambda i: send_list(spread(i, 3)))

    for which in range(3):
        loop(0, HEADS, lambda i: send(which, spread(i, 3)))

    def wait_for(ref, sem):
        pltpu.make_async_copy(ref, ref, sem).wait()

    @pl.when(active)
    def _():
        def block(which, place, half=None):
            low, size = (0, SRC) if half is None else (half * HALF, HALF)
            return held[which].at[pl.ds(place * SRC + low, size)]

        def swap(which, src, dst, i, dev, half=None):
            return pltpu.make_async_remote_copy(
                block(which, src, half), block(which, dst, half), b_send.at[which, i], b_recv.at[which, i],
                device_id=dev, device_id_type=MESH,
            )

        q_copies = [swap(0, 0, r, r - 1, q_peers[r - 1]) for r in range(1, 4)]
        y_copies = [[swap(which, 0, 2, half, y_peer, half) for half in range(2)] for which in (1, 2)]
        chip_copies = [swap(which, 0, 1, 2, chip_peer) for which in (1, 2)]
        on_copies = [[swap(which, 2, 3, 3 + half, chip_peer, half) for half in range(2)] for which in (1, 2)]

        def pass_on(i):
            for half in range(2):
                y_copies[i][half].wait_recv()
                on_copies[i][half].start()

        wait_for(block(0, 0), a_recv.at[0])
        for copy in q_copies:
            copy.start()

        wait_for(lists, a_recv.at[3])
        listed = lists[...]
        used[...] = jnp.broadcast_to(jnp.sum(jnp.where(listed >= 0, 1, 0), axis=2, keepdims=True), used.shape)
        listed = jnp.maximum(listed, 0)
        tile_yh = (listed >> 2) & 3
        tile_yl = ((listed >> 1) & 1) ^ jnp.where((tile_yh - yh) % 2 == 0, 1, 0)
        place = (tile_yl ^ yl) * 2 + ((listed & 1) ^ c)
        places[...] = place * SRC + tile_yh * 4 + (listed >> 4)
        to_scalars = pltpu.make_async_copy(places, places_s, list_sem)
        to_scalars.start()

        for which in (1, 2):
            wait_for(block(which, 0), a_recv.at[which])
            for copy in y_copies[which - 1]:
                copy.start()
            chip_copies[which - 1].start()
        pass_on(0)
        to_scalars.wait()
        for copy in q_copies + [chip_copies[0]] + on_copies[0]:
            copy.wait_recv()

        lane = lax.broadcasted_iota(jnp.int32, (D, D), 1)
        key_slot = lax.broadcasted_iota(jnp.int32, (1, 256), 1) % D // ROWS
        ones = jnp.ones((256, D), BF16)

        def gathered(which, t, g):
            blocks = [places_s[t, 0, s] for s in range(g * 8, g * 8 + 8)]
            return jnp.concatenate([held[which][b + half * HALF] for half in range(2) for b in blocks], axis=0)

        def weights_of(ts):
            scores = []
            for t in ts:
                limit = jnp.concatenate([used[t], used[t]], axis=1)
                query = jnp.concatenate([q_rows[r * SRC + half * HALF + t] for r in range(4) for half in range(2)], axis=0)
                scores.append([
                    lax.dot_general(query, gathered(1, t, g), (((1,), (1,)), ((), ())), preferred_element_type=F32)
                    + jnp.where(key_slot + g * 8 < limit, 0.0, LOW)
                    for g in range(4)
                ])
            found = []
            stats = stat[ts[0] // 8]
            for t, s in zip(ts, scores):
                top = jnp.maximum(jnp.maximum(s[0], s[1]), jnp.maximum(s[2], s[3]))
                top = jnp.max(top, axis=1, keepdims=True)
                stats = jnp.where(lane == t % 8, top, stats)
                found.append([jnp.exp2((s[g] - top) * SCALE).astype(BF16) for g in range(4)])
            stat[ts[0] // 8] = stats
            return found

        def numerators(ts, found):
            totals = []
            for t, w in zip(ts, found):
                total = jnp.zeros((D, 2 * D), F32)
                for g in range(4):
                    values = jnp.concatenate([gathered(2, t, g), ones], axis=1)
                    total = total + jnp.dot(w[g], values, preferred_element_type=F32)
                totals.append(total)
            stats = stat[ts[0] // 8]
            for t, total in zip(ts, totals):
                stats = jnp.where(lane == t % 8 + 64, total[:, D:], stats)
                numerator = total[:, :D].astype(BF16)
                for r in range(4):
                    for half in range(2):
                        low = r * PART + half * ROWS
                        part[r, half, t] = numerator[low : low + ROWS]
            stat[ts[0] // 8] = stats

        def part_copy(k, r):
            rows = pl.ds(k * PER_CHUNK, PER_CHUNK)
            return pltpu.make_async_remote_copy(
                part.at[r, :, rows], got.at[r - 1, :, rows], d_send.at[k, r - 1], d_recv.at[k, r - 1],
                device_id=q_peers[r - 1], device_id_type=MESH,
            )

        def pair(k):
            return [2 * k, 2 * k + 1]

        def send_parts(k):
            for r in range(1, 4):
                part_copy(k, r).start()

        def early_weights(k):
            for t, w in zip(pair(k), weights_of(pair(k))):
                for g in range(4):
                    kept[t, g] = w[g]

        def early_chunk(k):
            numerators(pair(k), [[kept[t, g] for g in range(4)] for t in pair(k)])
            send_parts(k)

        def chunk(k):
            numerators(pair(k), weights_of(pair(k)))
            send_parts(k)

        loop(0, EARLY // 2, early_weights)
        pass_on(1)
        loop(EARLY // 2, EARLY, early_weights)
        for copy in [chip_copies[1]] + on_copies[1]:
            copy.wait_recv()
        stat_copies = [
            [
                pltpu.make_async_remote_copy(
                    stat.at[g, pl.ds(r * PART, PART), :], got_stat.at[r - 1, g], s_send.at[g, r - 1], s_recv.at[g, r - 1],
                    device_id=q_peers[r - 1], device_id_type=MESH,
                )
                for r in range(1, 4)
            ]
            for g in range(2)
        ]
        loop(0, EARLY, early_chunk)
        for copy in stat_copies[0]:
            copy.start()
        loop(EARLY, CHUNKS, chunk)
        for copy in stat_copies[1]:
            copy.start()

        columns = out_ref.at[:, pl.ds(pl.multiple_of(head * D, D), D)]
        for k in range(CHUNKS):
            if k % 4 == 0:
                g = k // 4
                for copy in stat_copies[g]:
                    copy.wait_recv()
                stats = [stat[g, 0:PART, :]] + [got_stat[r, g] for r in range(3)]
                highest = jnp.maximum(jnp.maximum(stats[0], stats[1]), jnp.maximum(stats[2], stats[3]))
                factors = [jnp.exp2((s - highest) * SCALE) for s in stats]
                denominator = sum(f[:, 0:8] * s[:, 64:72] for f, s in zip(factors, stats))
                factors = [f[:, 0:8] / denominator for f in factors]
            for r in range(1, 4):
                part_copy(k, r).wait_recv()
            for t in pair(k):
                for half in range(2):
                    s = half * HALF + t
                    rows = slice(half * ROWS, (half + 1) * ROWS)
                    terms = [part[0, half, t]] + [got[r, half, t] for r in range(3)]
                    fin[s] = sum(f[rows, t % 8 : t % 8 + 1] * a.astype(F32) for f, a in zip(factors, terms)).astype(BF16)
                    pltpu.make_async_remote_copy(
                        fin.at[s], columns, e_sem.at[0], e_sem.at[1], device_id=source(s), device_id_type=MESH
                    ).start()

        for copy in q_copies + y_copies[0] + y_copies[1] + chip_copies + on_copies[0] + on_copies[1] + stat_copies[0] + stat_copies[1]:
            copy.wait_send()
        for k in range(CHUNKS):
            for r in range(1, 4):
                part_copy(k, r).wait_send()
        wait_for(fin, e_sem.at[0])

    for which in range(3):
        wait_for(rows_in[which], a_send.at[which])
    wait_for(out_ref, e_sem.at[1])

    @pl.when(xh == 0)
    def _():
        wait_for(list_room, a_send.at[3])


def per_device(query, key, value, tile_list):
    dma = pltpu.SemaphoreType.DMA
    return pl.pallas_call(
        kernel,
        out_shape=jax.ShapeDtypeStruct(query.shape, BF16),
        in_specs=[pl.BlockSpec(memory_space=pltpu.HBM)] * 3 + [pl.BlockSpec(memory_space=pltpu.VMEM)],
        out_specs=pl.BlockSpec(memory_space=pl.ANY),
        scratch_shapes=[
            pltpu.VMEM((1, D), jnp.int32),
            pltpu.VMEM((HEADS, 1, D), jnp.int32),
            pltpu.VMEM((TILES, 1, D), jnp.int32),
            pltpu.VMEM((TILES, 1, D), jnp.int32),
            pltpu.VMEM((TILES, 1, D), jnp.int32),
            pltpu.SMEM((TILES, 1, D), jnp.int32),
            pltpu.VMEM((4 * SRC, ROWS, D), BF16),
            pltpu.VMEM((4 * SRC, ROWS, D), BF16),
            pltpu.VMEM((4 * SRC, ROWS, D), BF16),
            pltpu.VMEM((2 * EARLY, 4, D, 256), BF16),
            pltpu.VMEM((4, 2, TILES, ROWS, D), BF16),
            pltpu.VMEM((3, 2, TILES, ROWS, D), BF16),
            pltpu.VMEM((2, D, D), F32),
            pltpu.VMEM((3, 2, PART, D), F32),
            pltpu.VMEM((SRC, ROWS, D), BF16),
            dma, dma((4,)), dma((4,)), dma((3, 5)), dma((3, 5)),
            dma((CHUNKS, 3)), dma((CHUNKS, 3)), dma((2, 3)), dma((2, 3)), dma((2,)),
        ],
        compiler_params=pltpu.CompilerParams(
            collective_id=0, has_side_effects=True, vmem_limit_bytes=56 * 1024 * 1024
        ),
        name="attention",
    )(query, key, value, tile_list)


def solution(mesh):
    rows = P(("blk", "uly"), None)
    return jax.shard_map(
        per_device,
        mesh=mesh,
        in_specs=(rows, rows, rows, P("blk", None)),
        out_specs=rows,
        check_vma=False,
    )
```

time: 58.1 us -> 54.1 us (0.931)
  the two profiles are of different devices: /device:TPU:1 before, /device:TPU:56 now
where the time goes in v3:
time: 54.1 us; the launch traced here: 53.9 us
  Pallas kernels  52.4 us (97%)
  local copies, waits for them, and re-layouts  1.54 us (3%)
    pallas_call x1, Pallas kernels, per_device(): pl.pallas_call(kernel, out_shape=jax.ShapeDtypeStruct(query.shape, BF16),...  52.4 us
    unnamed x1, local copies, waits for them, and re-layouts  1.54 us

profile of v3, /device:TPU:56, one launch (start us, length us, event | category | flops | bytes accessed | tf_op | source)
XLA Modules:
  0.0 53.9 jit_solution(3963896770591717539)
XLA Ops:
  0.0 52.4 %attention.1 = bf16[16,3072]{1,0:T(8,128)(2,1)} custom-call(bf16[16,3072]{1,0:T(8,128)(2,1)} %q_hbm.1, bf16[16,3072]{1,0:T(8,128)(2,1)} %k_hbm.1, bf16[16,3072]{1,0:T(8,128)(2,1)} %v_hbm.1, s32[1,32]{1,0:T(1,128)} %list_ref.1), custom_call_target="tpu_custom_call" | custom-call | tf_op jit(solution)/shard_map/attention/pallas_call | solution.py:307
  52.4 1.5 %copy.6 = bf16[16,3072]{1,0:T(8,128)(2,1)} copy(bf16[16,3072]{1,0:T(8,128)(2,1)} %attention.1) | data formatting | bytes 196608

commit v4 on v3

--- a/solution.py
+++ b/solution.py
@@ -15,7 +15,6 @@
 SLOTS = 32
 PART = 32
 CHUNKS = 8
-EARLY = 4
 PER_CHUNK = 2
 SCALE = 1.4426950408889634 / 128**0.5
 LOW = -1e30
@@ -24,7 +23,7 @@
 
 def kernel(
     q_hbm, k_hbm, v_hbm, list_ref, out_ref,
-    list_src, list_room, lists, used, places, places_s, q_rows, k_rows, v_rows, kept, part, got, stat, got_stat, fin,
+    list_room, lists, used, places, places_s, q_rows, k_rows, v_rows, part, got, stat, packed, got_stat, fin,
     list_sem, a_send, a_recv, b_send, b_recv, d_send, d_recv, s_send, s_recv, e_sem,
 ):
     blk, uly = lax.axis_index("blk"), lax.axis_index("uly")
@@ -85,8 +84,6 @@
             greet(peer)
         loop(0, SRC, lambda s: greet(source(s)))
 
-    list_src[...] = jnp.full_like(list_src, -1)
-    list_src[:, 0:SLOTS] = list_ref[...]
     stat[...] = jnp.zeros_like(stat)
 
     def spread(i, zcs):
@@ -100,7 +97,7 @@
 
     def send_list(h):
         pltpu.make_async_remote_copy(
-            list_src, lists.at[tile], a_send.at[3], a_recv.at[3], device_id=target(h), device_id_type=MESH
+            list_ref, lists.at[tile], a_send.at[3], a_recv.at[3], device_id=target(h), device_id_type=MESH
         ).start()
 
     @pl.when(active)
@@ -166,6 +163,10 @@
         pass_on(0)
         to_scalars.wait()
         for copy in q_copies + [chip_copies[0]] + on_copies[0]:
+            copy.wait_recv()
+
+        pass_on(1)
+        for copy in [chip_copies[1]] + on_copies[1]:
             copy.wait_recv()
 
         lane = lax.broadcasted_iota(jnp.int32, (D, D), 1)
@@ -206,7 +207,7 @@
                 totals.append(total)
             stats = stat[ts[0] // 8]
             for t, total in zip(ts, totals):
-                stats = jnp.where(lane == t % 8 + 64, total[:, D:], stats)
+                stats = jnp.where(lane == t % 8 + 8, total[:, D:], stats)
                 numerator = total[:, :D].astype(BF16)
                 for r in range(4):
                     for half in range(2):
@@ -228,40 +229,34 @@
             for r in range(1, 4):
                 part_copy(k, r).start()
 
-        def early_weights(k):
-            for t, w in zip(pair(k), weights_of(pair(k))):
-                for g in range(4):
-                    kept[t, g] = w[g]
-
-        def early_chunk(k):
-            numerators(pair(k), [[kept[t, g] for g in range(4)] for t in pair(k)])
-            send_parts(k)
-
         def chunk(k):
             numerators(pair(k), weights_of(pair(k)))
             send_parts(k)
 
-        loop(0, EARLY // 2, early_weights)
-        pass_on(1)
-        loop(EARLY // 2, EARLY, early_weights)
-        for copy in [chip_copies[1]] + on_copies[1]:
-            copy.wait_recv()
         stat_copies = [
             [
                 pltpu.make_async_remote_copy(
-                    stat.at[g, pl.ds(r * PART, PART), :], got_stat.at[r - 1, g], s_send.at[g, r - 1], s_recv.at[g, r - 1],
+                    packed.at[r, g], got_stat.at[r - 1, g], s_send.at[g, r - 1], s_recv.at[g, r - 1],
                     device_id=q_peers[r - 1], device_id_type=MESH,
                 )
                 for r in range(1, 4)
             ]
             for g in range(2)
         ]
-        loop(0, EARLY, early_chunk)
-        for copy in stat_copies[0]:
-            copy.start()
-        loop(EARLY, CHUNKS, chunk)
-        for copy in stat_copies[1]:
-            copy.start()
+
+        def pack(g):
+            for r in range(1, 4):
+                parts = [stat[g, r * PART + 8 * i : r * PART + 8 * (i + 1), 0:32] for i in range(4)]
+                packed[r, g] = jnp.concatenate(parts, axis=1)
+
+        def unpacked(block):
+            return jnp.concatenate([block[:, 32 * i : 32 * i + 16] for i in range(4)], axis=0)
+
+        for g in range(2):
+            loop(g * 4, g * 4 + 4, chunk)
+            pack(g)
+            for copy in stat_copies[g]:
+                copy.start()
 
         columns = out_ref.at[:, pl.ds(pl.multiple_of(head * D, D), D)]
         for k in range(CHUNKS):
@@ -269,10 +264,10 @@
                 g = k // 4
                 for copy in stat_copies[g]:
                     copy.wait_recv()
-                stats = [stat[g, 0:PART, :]] + [got_stat[r, g] for r in range(3)]
+                stats = [stat[g, 0:PART, 0:16]] + [unpacked(got_stat[r, g]) for r in range(3)]
                 highest = jnp.maximum(jnp.maximum(stats[0], stats[1]), jnp.maximum(stats[2], stats[3]))
                 factors = [jnp.exp2((s - highest) * SCALE) for s in stats]
-                denominator = sum(f[:, 0:8] * s[:, 64:72] for f, s in zip(factors, stats))
+                denominator = sum(f[:, 0:8] * s[:, 8:16] for f, s in zip(factors, stats))
                 factors = [f[:, 0:8] / denominator for f in factors]
             for r in range(1, 4):
                 part_copy(k, r).wait_recv()
@@ -307,29 +302,28 @@
     return pl.pallas_call(
         kernel,
         out_shape=jax.ShapeDtypeStruct(query.shape, BF16),
-        in_specs=[pl.BlockSpec(memory_space=pltpu.HBM)] * 3 + [pl.BlockSpec(memory_space=pltpu.VMEM)],
+        in_specs=[pl.BlockSpec(memory_space=pl.ANY)] * 4,
         out_specs=pl.BlockSpec(memory_space=pl.ANY),
         scratch_shapes=[
-            pltpu.VMEM((1, D), jnp.int32),
-            pltpu.VMEM((HEADS, 1, D), jnp.int32),
+            pltpu.VMEM((HEADS, 1, SLOTS), jnp.int32),
+            pltpu.VMEM((TILES, 1, SLOTS), jnp.int32),
             pltpu.VMEM((TILES, 1, D), jnp.int32),
-            pltpu.VMEM((TILES, 1, D), jnp.int32),
-            pltpu.VMEM((TILES, 1, D), jnp.int32),
-            pltpu.SMEM((TILES, 1, D), jnp.int32),
+            pltpu.VMEM((TILES, 1, SLOTS), jnp.int32),
+            pltpu.SMEM((TILES, 1, SLOTS), jnp.int32),
             pltpu.VMEM((4 * SRC, ROWS, D), BF16),
             pltpu.VMEM((4 * SRC, ROWS, D), BF16),
             pltpu.VMEM((4 * SRC, ROWS, D), BF16),
-            pltpu.VMEM((2 * EARLY, 4, D, 256), BF16),
             pltpu.VMEM((4, 2, TILES, ROWS, D), BF16),
             pltpu.VMEM((3, 2, TILES, ROWS, D), BF16),
             pltpu.VMEM((2, D, D), F32),
-            pltpu.VMEM((3, 2, PART, D), F32),
+            pltpu.VMEM((4, 2, 8, D), F32),
+            pltpu.VMEM((3, 2, 8, D), F32),
             pltpu.VMEM((SRC, ROWS, D), BF16),
             dma, dma((4,)), dma((4,)), dma((3, 5)), dma((3, 5)),
             dma((CHUNKS, 3)), dma((CHUNKS, 3)), dma((2, 3)), dma((2, 3)), dma((2,)),
         ],
         compiler_params=pltpu.CompilerParams(
-            collective_id=0, has_side_effects=True, vmem_limit_bytes=56 * 1024 * 1024
+            collective_id=0, has_side_effects=True, vmem_limit_bytes=56393728
         ),
         name="attention",
     )(query, key, value, tile_list)

time: 54.1 us -> 52.8 us (0.976)
  the two profiles are of different devices: /device:TPU:56 before, /device:TPU:1 now
where the time goes in v4:
time: 52.8 us; the launch traced here: 51.9 us
  Pallas kernels  50.6 us (96%)
  local copies, waits for them, and re-layouts  1.3 us (2%)
    pallas_call x1, Pallas kernels, per_device(): pl.pallas_call(kernel, out_shape=jax.ShapeDtypeStruct(query.shape, BF16),...  50.6 us
    unnamed x3, local copies, waits for them, and re-layouts  1.3 us

profile of v4, /device:TPU:1, one launch (start us, length us, event | category | flops | bytes accessed | tf_op | source)
XLA Modules:
  0.0 51.9 jit_solution(10204187617348431371)
XLA Ops:
  0.0 0.0 copy-start
  0.0 0.7 %copy-done = s32[1,32]{1,0:T(1,128)S(1)} copy-done((s32[1,32]{1,0:T(1,128)S(1)}, s32[1,32]{1,0:T(1,128)}, u32[]{:S(2)}) %copy-start) | copy-done | bytes 152
  0.7 50.6 %attention.1 = bf16[16,3072]{1,0:T(8,128)(2,1)S(1)} custom-call(bf16[16,3072]{1,0:T(8,128)(2,1)} %q_hbm.1, bf16[16,3072]{1,0:T(8,128)(2,1)} %k_hbm.1, bf16[16,3072]{1,0:T(8,128)(2,1)} %v_hbm.1, s32[1,32]{1,0:T(1,128)S(1)} %copy-done), custom_call_target="tpu_custom_call" | custom-call | tf_op jit(solution)/shard_map/attention/pallas_call | solution.py:302
  51.2 0.6 %copy.6 = bf16[16,3072]{1,0:T(8,128)(2,1)} copy(bf16[16,3072]{1,0:T(8,128)(2,1)S(1)} %attention.1) | data formatting | bytes 196608
Async XLA Ops:
  0.0 0.7 %copy-start = (s32[1,32]{1,0:T(1,128)S(1)}, s32[1,32]{1,0:T(1,128)}, u32[]{:S(2)}) copy-start(s32[1,32]{1,0:T(1,128)} %list_ref.1) | copy-start | bytes 388

commit v5 on v4

--- a/solution.py
+++ b/solution.py
@@ -49,11 +49,11 @@
     from_z = 4 * jnp.where(zc == 0, 1 - zr, zr)
 
     def source(s):
-        sxh, syh = s // 16, s // 4 % 4
-        return device(2 * sxh + crossed(sxh), 2 * syh + turned(syh), from_z + s % 4)
+        sxh, syh = s // 16, s % 4
+        return device(2 * sxh + crossed(sxh), 2 * syh + turned(syh), from_z + s // 4 % 4)
 
     head = zc * 8 + xh * 4 + yh
-    tile = yh * 4 + z % 4
+    tile = z % 4 * 4 + yh
     mine = xh * HALF + tile
 
     rows_in = (q_hbm, k_hbm, v_hbm)
@@ -151,7 +151,7 @@
         tile_yh = (listed >> 2) & 3
         tile_yl = ((listed >> 1) & 1) ^ jnp.where((tile_yh - yh) % 2 == 0, 1, 0)
         place = (tile_yl ^ yl) * 2 + ((listed & 1) ^ c)
-        places[...] = place * SRC + tile_yh * 4 + (listed >> 4)
+        places[...] = place * SRC + (listed >> 4) * 4 + tile_yh
         to_scalars = pltpu.make_async_copy(places, places_s, list_sem)
         to_scalars.start()
 

time: 52.8 us -> 51.9 us (0.983); the launches traced: 51.9 us -> 51.8 us
  no operation moved by 1% of the time
where the time goes in v5:
time: 51.9 us; the launch traced here: 51.8 us
  Pallas kernels  50.4 us (97%)
  local copies, waits for them, and re-layouts  1.3 us (3%)
    pallas_call x1, Pallas kernels, per_device(): pl.pallas_call(kernel, out_shape=jax.ShapeDtypeStruct(query.shape, BF16),...  50.4 us
    unnamed x3, local copies, waits for them, and re-layouts  1.3 us

profile of v5, /device:TPU:1, one launch (start us, length us, event | category | flops | bytes accessed | tf_op | source)
XLA Modules:
  0.0 51.8 jit_solution(6802425572403771771)
XLA Ops:
  0.0 0.0 copy-start
  0.0 0.7 %copy-done = s32[1,32]{1,0:T(1,128)S(1)} copy-done((s32[1,32]{1,0:T(1,128)S(1)}, s32[1,32]{1,0:T(1,128)}, u32[]{:S(2)}) %copy-start) | copy-done | bytes 152
  0.7 50.4 %attention.1 = bf16[16,3072]{1,0:T(8,128)(2,1)S(1)} custom-call(bf16[16,3072]{1,0:T(8,128)(2,1)} %q_hbm.1, bf16[16,3072]{1,0:T(8,128)(2,1)} %k_hbm.1, bf16[16,3072]{1,0:T(8,128)(2,1)} %v_hbm.1, s32[1,32]{1,0:T(1,128)S(1)} %copy-done), custom_call_target="tpu_custom_call" | custom-call | tf_op jit(solution)/shard_map/attention/pallas_call | solution.py:302
  51.1 0.6 %copy.6 = bf16[16,3072]{1,0:T(8,128)(2,1)} copy(bf16[16,3072]{1,0:T(8,128)(2,1)S(1)} %attention.1) | data formatting | bytes 196608
Async XLA Ops:
  0.0 0.7 %copy-start = (s32[1,32]{1,0:T(1,128)S(1)}, s32[1,32]{1,0:T(1,128)}, u32[]{:S(2)}) copy-start(s32[1,32]{1,0:T(1,128)} %list_ref.1) | copy-start | bytes 388

commit v6 on v5

--- a/solution.py
+++ b/solution.py
@@ -108,12 +108,12 @@
     def _():
         pl.semaphore_wait(barrier, HEADS)
 
-    @pl.when(xh == 0)
-    def _():
-        loop(0, HEADS, lambda i: send_list(spread(i, 3)))
-
     for which in range(3):
         loop(0, HEADS, lambda i: send(which, spread(i, 3)))
+
+    @pl.when(xh == 0)
+    def _():
+        loop(0, HEADS, lambda i: send_list(spread(i, 3)))
 
     def wait_for(ref, sem):
         pltpu.make_async_copy(ref, ref, sem).wait()
@@ -143,6 +143,12 @@
         wait_for(block(0, 0), a_recv.at[0])
         for copy in q_copies:
             copy.start()
+
+        for which in (1, 2):
+            wait_for(block(which, 0), a_recv.at[which])
+            for copy in y_copies[which - 1]:
+                copy.start()
+            chip_copies[which - 1].start()
 
         wait_for(lists, a_recv.at[3])
         listed = lists[...]
@@ -155,11 +161,6 @@
         to_scalars = pltpu.make_async_copy(places, places_s, list_sem)
         to_scalars.start()
 
-        for which in (1, 2):
-            wait_for(block(which, 0), a_recv.at[which])
-            for copy in y_copies[which - 1]:
-                copy.start()
-            chip_copies[which - 1].start()
         pass_on(0)
         to_scalars.wait()
         for copy in q_copies + [chip_copies[0]] + on_copies[0]:

time: 51.9 us -> 50.8 us (0.979)
  Pallas kernels: 50.4 us -> 49.4 us
    pallas_call x1, Pallas kernels: 50.4 us -> 49.4 us  [per_device(): pl.pallas_call(kernel, out_shape=jax.ShapeDtypeStruct(query.shape, BF16),...]
where the time goes in v6:
time: 50.8 us; the launch traced here: 50.7 us
  Pallas kernels  49.4 us (97%)
  local copies, waits for them, and re-layouts  1.3 us (3%)
    pallas_call x1, Pallas kernels, per_device(): pl.pallas_call(kernel, out_shape=jax.ShapeDtypeStruct(query.shape, BF16),...  49.4 us
    unnamed x3, local copies, waits for them, and re-layouts  1.3 us

profile of v6, /device:TPU:1, one launch (start us, length us, event | category | flops | bytes accessed | tf_op | source)
XLA Modules:
  0.0 50.7 jit_solution(5254852525000325597)
XLA Ops:
  0.0 0.0 copy-start
  0.0 0.7 %copy-done = s32[1,32]{1,0:T(1,128)S(1)} copy-done((s32[1,32]{1,0:T(1,128)S(1)}, s32[1,32]{1,0:T(1,128)}, u32[]{:S(2)}) %copy-start) | copy-done | bytes 152
  0.7 49.4 %attention.1 = bf16[16,3072]{1,0:T(8,128)(2,1)S(1)} custom-call(bf16[16,3072]{1,0:T(8,128)(2,1)} %q_hbm.1, bf16[16,3072]{1,0:T(8,128)(2,1)} %k_hbm.1, bf16[16,3072]{1,0:T(8,128)(2,1)} %v_hbm.1, s32[1,32]{1,0:T(1,128)S(1)} %copy-done), custom_call_target="tpu_custom_call" | custom-call | tf_op jit(solution)/shard_map/attention/pallas_call | solution.py:303
  50.1 0.6 %copy.6 = bf16[16,3072]{1,0:T(8,128)(2,1)} copy(bf16[16,3072]{1,0:T(8,128)(2,1)S(1)} %attention.1) | data formatting | bytes 196608
Async XLA Ops:
  0.0 0.7 %copy-start = (s32[1,32]{1,0:T(1,128)S(1)}, s32[1,32]{1,0:T(1,128)}, u32[]{:S(2)}) copy-start(s32[1,32]{1,0:T(1,128)} %list_ref.1) | copy-start | bytes 388

commit v7 on v6

--- a/solution.py
+++ b/solution.py
@@ -87,7 +87,7 @@
     stat[...] = jnp.zeros_like(stat)
 
     def spread(i, zcs):
-        return (jnp.where(zc < 2, 2, 0) + i // 8) % zcs * 8 + (xh + 1 + i // 4) % 2 * 4 + (yh + 2 + i) % 4
+        return (jnp.where(zc < 2, 2, 0) + i // 4) % zcs * 8 + (xh + 1 + i // 12) % 2 * 4 + (yh + 2 + i) % 4
 
     def send(which, h):
         pltpu.make_async_remote_copy(

time: 50.8 us -> 50.8 us (level)
  no operation moved by 1% of the time
where the time goes in v7:
time: 50.8 us; the launch traced here: 50.7 us
  Pallas kernels  49.3 us (97%)
  local copies, waits for them, and re-layouts  1.3 us (3%)
    pallas_call x1, Pallas kernels, per_device(): pl.pallas_call(kernel, out_shape=jax.ShapeDtypeStruct(query.shape, BF16),...  49.3 us
    unnamed x3, local copies, waits for them, and re-layouts  1.3 us

profile of v7, /device:TPU:1, one launch (start us, length us, event | category | flops | bytes accessed | tf_op | source)
XLA Modules:
  0.0 50.7 jit_solution(8360713580179534)
XLA Ops:
  0.0 0.0 copy-start
  0.0 0.7 %copy-done = s32[1,32]{1,0:T(1,128)S(1)} copy-done((s32[1,32]{1,0:T(1,128)S(1)}, s32[1,32]{1,0:T(1,128)}, u32[]{:S(2)}) %copy-start) | copy-done | bytes 152
  0.7 49.3 %attention.1 = bf16[16,3072]{1,0:T(8,128)(2,1)S(1)} custom-call(bf16[16,3072]{1,0:T(8,128)(2,1)} %q_hbm.1, bf16[16,3072]{1,0:T(8,128)(2,1)} %k_hbm.1, bf16[16,3072]{1,0:T(8,128)(2,1)} %v_hbm.1, s32[1,32]{1,0:T(1,128)S(1)} %copy-done), custom_call_target="tpu_custom_call" | custom-call | tf_op jit(solution)/shard_map/attention/pallas_call | solution.py:303
  50.0 0.6 %copy.6 = bf16[16,3072]{1,0:T(8,128)(2,1)} copy(bf16[16,3072]{1,0:T(8,128)(2,1)S(1)} %attention.1) | data formatting | bytes 196608
Async XLA Ops:
  0.0 0.7 %copy-start = (s32[1,32]{1,0:T(1,128)S(1)}, s32[1,32]{1,0:T(1,128)}, u32[]{:S(2)}) copy-start(s32[1,32]{1,0:T(1,128)} %list_ref.1) | copy-start | bytes 388
